TPU v7x, 32 devices: a whole 2x2x4 slice. The times are simulated.
32 devices in a mesh: member: 2 (over core), tile: 16 (over z, y, x).
Axes of the slice: x: 2, y: 2, z: 4, core: 2. Of those that a mesh axis runs over, the one named last changes fastest.
Arguments:
- parent_state: float32 [4, 81, 128, 128], P('member', None, 'tile'), may hold values from -6 to 6
- nest_state: float32 [4, 81, 4096], P('member', None, 'tile'), may hold values from -6 to 6
- terrain: int32 [128, 128], P('tile'), may hold values from 0 to 3000
- shift_x: int32 [4], replicated, may hold values from -16 to 16
- boundary_index: int32 [4, 256], P(None, 'tile'), may hold values from 0 to 16383, as said below
- reloc_dest: int32 [4, 4096], P(None, 'tile'), may hold values from 0 to 4095, as said below
Outputs:
- parent_out: float32 [4, 81, 128, 128], P('member', None, 'tile')
- nest_out: float32 [4, 81, 4096], P('member', None, 'tile')
- nest_mean: float32 [81, 4096], P(None, 'tile')
- nest_variance: float32 [81, 4096], P(None, 'tile')
Inputs may be any that keep to these rules, and one draw needn't show every extreme that they name: `boundary_index`: for each step and nest tile t, entries t * 16 to t * 16 + 15 come in 8 runs of 2; each run lies on one parent tile (rows of 8), different runs of one tile on different parent tiles, and the cells within one run differ. `reloc_dest`: for each step a permutation of the 4096 nest columns. The columns of one tile go in runs of 32 (slots g * 32 to g * 32 + 31) each wholly to one tile, into that tile's run g; the runs of one tile go to 8 different tiles, so exactly 32 or no columns pass from one tile to another.
All inputs are finite; a program needn't handle non-finite values.
Results may differ from a plain program's by a relative error of at most 0.00047.
Values may be sent and summed in bfloat16 or wider, within the bound.
A program may use at most 64 MiB of HBM per device.

v0:
```python
import jax
import jax.numpy as jnp
from jax import lax
from jax.sharding import PartitionSpec as P

CAPB = 2
STEPS = 4


HORIZ_MIX = 0.15
VERT_MIX = 0.1
DRAG_RATE = 0.1
RELAX_RATE = 0.5
IMPLICIT_MIX = 0.8


def with_halo(block, sides, width):
    for axis, dim in sides:
        count = lax.axis_size(axis)
        forward = [(i, i + 1) for i in range(count - 1)]
        backward = [(target, source) for source, target in forward]
        low = lax.ppermute(
            lax.slice_in_dim(block, block.shape[dim] - width, None, axis=dim), axis, forward
        )
        high = lax.ppermute(lax.slice_in_dim(block, 0, width, axis=dim), axis, backward)
        block = jnp.concatenate([low, block, high], axis=dim)
    return block


def parent_update(parent, damping):
    padded = with_halo(parent, (("tile", 2),), 1)
    north_row = padded[:, :, 2:, :]
    south_row = padded[:, :, :-2, :]
    east_cell = jnp.roll(parent, -1, axis=3)
    west_cell = jnp.roll(parent, 1, axis=3)
    upper_level = jnp.concatenate([parent[:, 1:], parent[:, -1:]], axis=1)
    lower_level = jnp.concatenate([parent[:, :1], parent[:, :-1]], axis=1)
    return (
        parent
        + HORIZ_MIX * (north_row + south_row + east_cell + west_cell - 4.0 * parent)
        + VERT_MIX * (upper_level + lower_level - 2.0 * parent)
        - damping * parent
    )


def implicit_column(column_field):
    levels = column_field.shape[1]
    pivots = []
    cprime = []
    previous = 0.0
    for level in range(levels):
        neighbours = (1 if level > 0 else 0) + (1 if level < levels - 1 else 0)
        diagonal = 1.0 + IMPLICIT_MIX * neighbours
        pivot = diagonal - IMPLICIT_MIX * previous if level > 0 else diagonal
        previous = IMPLICIT_MIX / pivot
        pivots.append(pivot)
        cprime.append(previous)
    sweep = []
    forward = None
    for level in range(levels):
        source = column_field[:, level]
        if level > 0:
            source = source + IMPLICIT_MIX * forward
        forward = source / pivots[level]
        sweep.append(forward)
    result = [None] * levels
    result[levels - 1] = sweep[levels - 1]
    for level in range(levels - 2, -1, -1):
        result[level] = sweep[level] + cprime[level] * result[level + 1]
    return jnp.stack(result, axis=1)


def locate(indices, shift_by, row_width, tile_cells):
    rows_at = indices // row_width
    cols_at = jnp.mod(indices % row_width + shift_by, row_width)
    moved = rows_at * row_width + cols_at
    return (moved // tile_cells, moved % tile_cells)


def on_device(parent_state, nest_state, terrain, shift_x, boundary_index, reloc_dest):
    members, levels, rows_here, row_width = parent_state.shape
    columns_here = nest_state.shape[2]
    tile_count = lax.axis_size("tile")
    tile_cells = rows_here * row_width
    boundary_here = boundary_index.shape[1]
    owners = boundary_here // CAPB
    mixed = members * levels
    groups = tile_count // 2
    per_peer = columns_here // groups
    damping = DRAG_RATE * terrain.astype(jnp.float32) / 3000.0
    parent = parent_state
    nest_field = nest_state
    for step_no in range(STEPS):
        flat_parent = parent.astype(jnp.bfloat16).reshape(mixed, tile_cells)
        offset = shift_x[step_no]
        owner_of, local_of = locate(boundary_index[step_no], offset, row_width, tile_cells)
        owner_runs = owner_of.reshape(owners, CAPB)[:, 0]
        local_runs = local_of.reshape(owners, CAPB)
        requests_out = jnp.zeros((tile_count, CAPB), jnp.int32).at[owner_runs].set(local_runs)
        values = jnp.transpose(
            jnp.take(
                flat_parent,
                lax.all_to_all(requests_out, "tile", split_axis=0, concat_axis=0, tiled=True),
                axis=1,
            ),
            (1, 2, 0),
        )
        received = lax.all_to_all(values, "tile", split_axis=0, concat_axis=0, tiled=True)
        edge_values = received[owner_runs].reshape(boundary_here, mixed)
        edge_values = (
            jnp.transpose(edge_values).astype(jnp.float32).reshape(members, levels, boundary_here)
        )
        edge_cols = nest_field[:, :, :boundary_here]
        edge_cols = edge_cols + RELAX_RATE * (edge_values - edge_cols)
        nest_field = jnp.concatenate([edge_cols, nest_field[:, :, boundary_here:]], axis=2)
        nest_field = implicit_column(nest_field)
        targets = reloc_dest[step_no].reshape(groups, per_peer)
        target_tile = targets[:, 0] // columns_here
        slots = targets % columns_here
        values_out = jnp.transpose(nest_field.reshape(mixed, groups, per_peer), (1, 2, 0))
        send_values = (
            jnp.zeros((tile_count, per_peer, mixed), jnp.float32).at[target_tile].set(values_out)
        )
        send_slots = (
            jnp.full((tile_count, per_peer), columns_here, jnp.int32).at[target_tile].set(slots)
        )
        got_values, got_slots = (
            lax.all_to_all(send_values, "tile", split_axis=0, concat_axis=0, tiled=True),
            lax.all_to_all(send_slots, "tile", split_axis=0, concat_axis=0, tiled=True),
        )
        placed = (
            jnp.zeros((columns_here, mixed), jnp.float32)
            .at[got_slots.reshape(-1)]
            .set(got_values.reshape(-1, mixed), mode="drop")
        )
        nest_field = jnp.transpose(placed).reshape(members, levels, columns_here)
        parent = parent_update(parent, damping)
    ensemble = members * lax.axis_size("member")
    totals = lax.psum(jnp.sum(nest_field, axis=0), "member")
    mean_field = totals / ensemble
    spread_sum = lax.psum(jnp.sum((nest_field - mean_field) ** 2, axis=0), "member")
    variance = spread_sum / ensemble
    return (parent, nest_field, mean_field, variance)


def solution(mesh):
    in_specs = (
        P("member", None, "tile", None),
        P("member", None, "tile"),
        P("tile", None),
        P(),
        P(None, "tile"),
        P(None, "tile"),
    )
    out_specs = (
        P("member", None, "tile", None),
        P("member", None, "tile"),
        P(None, "tile"),
        P(None, "tile"),
    )
    return jax.shard_map(
        on_device, mesh=mesh, in_specs=in_specs, out_specs=out_specs, check_vma=False
    )
```

profile of v0, /device:TPU:0, one launch (start us, length us, event | category | flops | bytes accessed | tf_op | source)
XLA Modules:
  0.0 338.0 jit_solution(450833958341519604)
XLA Ops:
  10.1 1.8 scatter_custom_fusion.4
  12.0 8.3 %all-to-all-start.4 = ((s32[16,1,2]{2,1,0:T(1,128)}), s32[16,1,2]{2,1,0:T(1,128)S(1)}, u32[]{:S(2)}, u32[]{:S(2)}) async-start(s32[16,1,2]{2,1,0:T(1,128)} %bitcast.512), calls=%async_computation.4 | async-start | bytes 16384 | tf_op jit(solution)/shard_map/all_to_all | solution.py:103
  23.6 5.2 %collective-permute-start.1 = (f32[2,81,1,128]{3,1,2,0:T(8,128)}, f32[2,81,1,128]{3,1,2,0:T(8,128)}, u32[]{:S(2)}, u32[]{:S(2)}) collective-permute-start(f32[2,81,1,128]{3,1,2,0:T(8,128)} %get-tuple-element.674), channel_id=1, source_target_pairs={{0,1},{1,2},{2,3},{3,4},{4,5},{5,6},{6,7},{7,8},{8,9},{9,10},{10,1... | collective-permute-start | bytes 248840 | tf_op jit(solution)/shard_map/ppermute | solution.py:22
  33.3 1.8 scatter_custom_fusion.7
  36.5 1.8 scatter_custom_fusion.10
  39.9 1.9 scatter_custom_fusion.13
  51.6 7.2 %all-to-all-start.7 = ((s32[16,1,2]{2,1,0:T(1,128)}), s32[16,1,2]{2,1,0:T(1,128)S(1)}, u32[]{:S(2)}, u32[]{:S(2)}) async-start(s32[16,1,2]{2,1,0:T(1,128)} %bitcast.514), calls=%async_computation.7 | async-start | bytes 16384 | tf_op jit(solution)/shard_map/all_to_all | solution.py:103
  59.4 6.6 %all-to-all-done.7 = s32[16,1,2]{2,1,0:T(1,128)S(1)} async-done(((s32[16,1,2]{2,1,0:T(1,128)}), s32[16,1,2]{2,1,0:T(1,128)S(1)}, u32[]{:S(2)}, u32[]{:S(2)}) %all-to-all-start.7) | async-done | bytes 160 | tf_op jit(solution)/shard_map/all_to_all | solution.py:103
  66.0 3.5 %all-to-all-start.10 = ((s32[16,1,2]{2,1,0:T(1,128)}), s32[16,1,2]{2,1,0:T(1,128)S(1)}, u32[]{:S(2)}, u32[]{:S(2)}) async-start(s32[16,1,2]{2,1,0:T(1,128)} %bitcast.516), calls=%async_computation.10 | async-start | bytes 16384 | tf_op jit(solution)/shard_map/all_to_all | solution.py:103
  71.5 5.2 %all-to-all-done.10 = s32[16,1,2]{2,1,0:T(1,128)S(1)} async-done(((s32[16,1,2]{2,1,0:T(1,128)}), s32[16,1,2]{2,1,0:T(1,128)S(1)}, u32[]{:S(2)}, u32[]{:S(2)}) %all-to-all-start.10) | async-done | bytes 160 | tf_op jit(solution)/shard_map/all_to_all | solution.py:103
  76.7 3.5 %all-to-all-start.13 = ((s32[16,1,2]{2,1,0:T(1,128)}), s32[16,1,2]{2,1,0:T(1,128)S(1)}, u32[]{:S(2)}, u32[]{:S(2)}) async-start(s32[16,1,2]{2,1,0:T(1,128)} %bitcast.518), calls=%async_computation.13 | async-start | bytes 16384 | tf_op jit(solution)/shard_map/all_to_all | solution.py:103
  82.3 5.1 %all-to-all-done.13 = s32[16,1,2]{2,1,0:T(1,128)S(1)} async-done(((s32[16,1,2]{2,1,0:T(1,128)}), s32[16,1,2]{2,1,0:T(1,128)S(1)}, u32[]{:S(2)}, u32[]{:S(2)}) %all-to-all-start.13) | async-done | bytes 160 | tf_op jit(solution)/shard_map/all_to_all | solution.py:103
  87.4 3.5 %all-to-all-start.3 = ((s32[16,1,32]{2,1,0:T(1,128)}), s32[16,1,32]{2,1,0:T(1,128)S(1)}, u32[]{:S(2)}, u32[]{:S(2)}) async-start(s32[16,1,32]{2,1,0:T(1,128)} %bitcast.11), calls=%async_computation.3 | async-start | bytes 16384 | tf_op jit(solution)/shard_map/all_to_all | solution.py:129
  91.7 6.4 %all-to-all-done.3 = s32[16,1,32]{2,1,0:T(1,128)S(1)} async-done(((s32[16,1,32]{2,1,0:T(1,128)}), s32[16,1,32]{2,1,0:T(1,128)S(1)}, u32[]{:S(2)}, u32[]{:S(2)}) %all-to-all-start.3) | async-done | bytes 2080 | tf_op jit(solution)/shard_map/all_to_all | solution.py:129
  98.2 3.5 %all-to-all-start.2 = ((s32[16,1,32]{2,1,0:T(1,128)}), s32[16,1,32]{2,1,0:T(1,128)S(1)}, u32[]{:S(2)}, u32[]{:S(2)}) async-start(s32[16,1,32]{2,1,0:T(1,128)} %bitcast.8), calls=%async_computation.2 | async-start | bytes 16384 | tf_op jit(solution)/shard_map/all_to_all | solution.py:129
  102.0 6.9 %all-to-all-done.2 = s32[16,1,32]{2,1,0:T(1,128)S(1)} async-done(((s32[16,1,32]{2,1,0:T(1,128)}), s32[16,1,32]{2,1,0:T(1,128)S(1)}, u32[]{:S(2)}, u32[]{:S(2)}) %all-to-all-start.2) | async-done | bytes 2080 | tf_op jit(solution)/shard_map/all_to_all | solution.py:129
  108.9 3.4 %all-to-all-start.1 = ((s32[16,1,32]{2,1,0:T(1,128)}), s32[16,1,32]{2,1,0:T(1,128)S(1)}, u32[]{:S(2)}, u32[]{:S(2)}) async-start(s32[16,1,32]{2,1,0:T(1,128)} %bitcast.5), calls=%async_computation.1 | async-start | bytes 16384 | tf_op jit(solution)/shard_map/all_to_all | solution.py:129
  116.3 3.2 all-to-all-done.1
  119.6 3.6 %all-to-all-start = ((s32[16,1,32]{2,1,0:T(1,128)}), s32[16,1,32]{2,1,0:T(1,128)S(1)}, u32[]{:S(2)}, u32[]{:S(2)}) async-start(s32[16,1,32]{2,1,0:T(1,128)} %bitcast.2), calls=%async_computation | async-start | bytes 16384 | tf_op jit(solution)/shard_map/all_to_all | solution.py:129
  124.6 5.9 %all-to-all-done = s32[16,1,32]{2,1,0:T(1,128)S(1)} async-done(((s32[16,1,32]{2,1,0:T(1,128)}), s32[16,1,32]{2,1,0:T(1,128)S(1)}, u32[]{:S(2)}, u32[]{:S(2)}) %all-to-all-start) | async-done | bytes 2080 | tf_op jit(solution)/shard_map/all_to_all | solution.py:129
  130.5 3.5 %all-to-all-start.5 = ((bf16[16,2,162]{2,1,0:T(2,128)(2,1)}), bf16[16,2,162]{2,1,0:T(2,128)(2,1)S(1)}, u32[]{:S(2)}, u32[]{:S(2)}) async-start(bf16[16,2,162]{2,1,0:T(2,128)(2,1)} %broadcast_select_fusion.3), calls=%async_computation.5 | async-start | bytes 32768 | tf_op jit(solution)/shard_map/all_to_all | solution.py:108
  137.4 3.9 %all-to-all-done.5 = bf16[16,2,162]{2,1,0:T(2,128)(2,1)S(1)} async-done(((bf16[16,2,162]{2,1,0:T(2,128)(2,1)}), bf16[16,2,162]{2,1,0:T(2,128)(2,1)S(1)}, u32[]{:S(2)}, u32[]{:S(2)}) %all-to-all-start.5) | async-done | bytes 10400 | tf_op jit(solution)/shard_map/all_to_all | solution.py:108
  145.8 2.2 scatter_fusion
  148.7 2.9 fusion.759
  158.2 3.5 %all-to-all-start.8 = ((bf16[16,2,162]{2,1,0:T(2,128)(2,1)}), bf16[16,2,162]{2,1,0:T(2,128)(2,1)S(1)}, u32[]{:S(2)}, u32[]{:S(2)}) async-start(bf16[16,2,162]{2,1,0:T(2,128)(2,1)} %broadcast_select_fusion.2), calls=%async_computation.8 | async-start | bytes 32768 | tf_op jit(solution)/shard_map/all_to_all | solution.py:108
  163.0 4.6 %collective-permute-start.3 = (f32[2,81,1,128]{3,1,2,0:T(8,128)S(1)}, f32[2,81,1,128]{3,1,2,0:T(8,128)S(1)}, u32[]{:S(2)}, u32[]{:S(2)}) collective-permute-start(f32[2,81,1,128]{3,1,2,0:T(8,128)S(1)} %copy-done.10), channel_id=1, source_target_pairs={{0,1},{1,2},{2,3},{3,4},{4,5},{5,6},{6,7},{7,8},{8,9},{9,10},{10,1... | collective-permute-start | bytes 248840 | tf_op jit(solution)/shard_map/ppermute | solution.py:22
  169.0 6.9 %all-to-all-start.6 = ((f32[16,32,162]{2,1,0:T(8,128)}), f32[16,32,162]{2,1,0:T(8,128)}, u32[]{:S(2)}, u32[]{:S(2)}) async-start(f32[16,32,162]{2,1,0:T(8,128)} %scatter_fusion), calls=%async_computation.6 | async-start | bytes 1048576 | tf_op jit(solution)/shard_map/all_to_all | solution.py:128
  178.2 2.9 fusion.680
  185.8 5.2 %collective-permute-start.5 = (f32[2,81,1,128]{3,1,2,0:T(8,128)}, f32[2,81,1,128]{3,1,2,0:T(8,128)}, u32[]{:S(2)}, u32[]{:S(2)}) collective-permute-start(f32[2,81,1,128]{3,1,2,0:T(8,128)} %get-tuple-element.654), channel_id=1, source_target_pairs={{0,1},{1,2},{2,3},{3,4},{4,5},{5,6},{6,7},{7,8},{8,9},{9,10},{10,1... | collective-permute-start | bytes 248840 | tf_op jit(solution)/shard_map/ppermute | solution.py:22
  193.3 7.2 %all-to-all-start.11 = ((bf16[16,2,162]{2,1,0:T(2,128)(2,1)}), bf16[16,2,162]{2,1,0:T(2,128)(2,1)}, u32[]{:S(2)}, u32[]{:S(2)}) async-start(bf16[16,2,162]{2,1,0:T(2,128)(2,1)} %broadcast_select_fusion.1), calls=%async_computation.11 | async-start | bytes 32768 | tf_op jit(solution)/shard_map/all_to_all | solution.py:108
  200.5 2.8 scatter_custom_fusion.6
  209.0 2.2 scatter_fusion.1
  211.2 6.9 %all-to-all-start.9 = ((f32[16,32,162]{2,1,0:T(8,128)}), f32[16,32,162]{2,1,0:T(8,128)}, u32[]{:S(2)}, u32[]{:S(2)}) async-start(f32[16,32,162]{2,1,0:T(8,128)} %scatter_fusion.1), calls=%async_computation.9 | async-start | bytes 1048576 | tf_op jit(solution)/shard_map/all_to_all | solution.py:128
  221.7 3.0 fusion.601
  229.1 6.0 %all-to-all-start.14 = ((bf16[16,2,162]{2,1,0:T(2,128)(2,1)}), bf16[16,2,162]{2,1,0:T(2,128)(2,1)S(1)}, u32[]{:S(2)}, u32[]{:S(2)}) async-start(bf16[16,2,162]{2,1,0:T(2,128)(2,1)} %broadcast_select_fusion), calls=%async_computation.14 | async-start | bytes 32768 | tf_op jit(solution)/shard_map/all_to_all | solution.py:108
  235.2 3.0 scatter_custom_fusion.9
  243.0 2.2 scatter_fusion.2
  245.2 6.9 %all-to-all-start.12 = ((f32[16,32,162]{2,1,0:T(8,128)}), f32[16,32,162]{2,1,0:T(8,128)S(1)}, u32[]{:S(2)}, u32[]{:S(2)}) async-start(f32[16,32,162]{2,1,0:T(8,128)} %scatter_fusion.2), calls=%async_computation.12 | async-start | bytes 1048576 | tf_op jit(solution)/shard_map/all_to_all | solution.py:128
  254.9 8.0 %all-to-all-done.12 = f32[16,32,162]{2,1,0:T(8,128)S(1)} async-done(((f32[16,32,162]{2,1,0:T(8,128)}), f32[16,32,162]{2,1,0:T(8,128)S(1)}, u32[]{:S(2)}, u32[]{:S(2)}) %all-to-all-start.12) | async-done | bytes 331808 | tf_op jit(solution)/shard_map/all_to_all | solution.py:128
  262.9 2.3 scatter_custom_fusion.12
  269.3 2.2 scatter_fusion.3
  271.5 4.1 %all-to-all-start.15 = ((f32[16,32,162]{2,1,0:T(8,128)}), f32[16,32,162]{2,1,0:T(8,128)S(1)}, u32[]{:S(2)}, u32[]{:S(2)}) async-start(f32[16,32,162]{2,1,0:T(8,128)} %scatter_fusion.3), calls=%async_computation.15 | async-start | bytes 1048576 | tf_op jit(solution)/shard_map/all_to_all | solution.py:128
  277.6 8.7 %all-to-all-done.15 = f32[16,32,162]{2,1,0:T(8,128)S(1)} async-done(((f32[16,32,162]{2,1,0:T(8,128)}), f32[16,32,162]{2,1,0:T(8,128)S(1)}, u32[]{:S(2)}, u32[]{:S(2)}) %all-to-all-start.15) | async-done | bytes 331808 | tf_op jit(solution)/shard_map/all_to_all | solution.py:128
  287.1 2.8 scatter_custom_fusion.15
  292.9 5.2 %collective-permute-start.7 = (f32[2,81,1,128]{3,1,2,0:T(8,128)S(1)}, f32[2,81,1,128]{3,1,2,0:T(8,128)}, u32[]{:S(2)}, u32[]{:S(2)}) collective-permute-start(f32[2,81,1,128]{3,1,2,0:T(8,128)S(1)} %get-tuple-element.652), channel_id=1, source_target_pairs={{0,1},{1,2},{2,3},{3,4},{4,5},{5,6},{6,7},{7,8},{8,9},{9,10},{10,1... | collective-permute-start | bytes 248840 | tf_op jit(solution)/shard_map/ppermute | solution.py:22
  298.1 9.6 %all-reduce.3.cloned.1.call-done = f32[81,256]{1,0:T(8,128)} async-done(((f32[81,256]{1,0:T(8,128)}), f32[81,256]{1,0:T(8,128)}) %all-reduce.3.cloned.1.call-update) | async-done | bytes 82960 | tf_op jit(solution)/shard_map/psum | solution.py:139
  309.3 2.2 fusion.7
  313.3 16.4 %all-reduce.5.cloned.1.call-done = f32[81,256]{1,0:T(8,128)} async-done(((f32[81,256]{1,0:T(8,128)}), f32[81,256]{1,0:T(8,128)}) %all-reduce.5.cloned.1.call-update) | async-done | bytes 82960 | tf_op jit(solution)/shard_map/psum | solution.py:141
  (600 shorter events, 96.7 us)
Async XLA Ops:
  12.0 39.6 %all-to-all-start.4 = ((s32[16,1,2]{2,1,0:T(1,128)}), s32[16,1,2]{2,1,0:T(1,128)S(1)}, u32[]{:S(2)}, u32[]{:S(2)}) async-start(s32[16,1,2]{2,1,0:T(1,128)} %bitcast.512), calls=%async_computation.4 | async-start | bytes 16384 | tf_op jit(solution)/shard_map/all_to_all | solution.py:103
  20.3 8.5 %copy-start.1 = (f32[2,81,8,128]{3,2,1,0:T(8,128)S(1)}, f32[2,81,8,128]{3,2,1,0:T(8,128)}, u32[]{:S(2)}) copy-start(f32[2,81,8,128]{3,2,1,0:T(8,128)} %param.8) | copy-start | bytes 1990660
  22.3 125.7 %collective-permute-start = (f32[2,81,1,128]{3,1,2,0:T(8,128)}, f32[2,81,1,128]{3,1,2,0:T(8,128)}, u32[]{:S(2)}, u32[]{:S(2)}) collective-permute-start(f32[2,81,1,128]{3,1,2,0:T(8,128)} %get-tuple-element.673), channel_id=1, source_target_pairs={{1,0},{2,1},{3,2},{4,3},{5,4},{6,5},{7,6},{8,7},{9,8},{10,9},{11,1... | collective-permute-start | bytes 248840 | tf_op jit(solution)/shard_map/ppermute | solution.py:25
  23.6 124.4 %collective-permute-start.1 = (f32[2,81,1,128]{3,1,2,0:T(8,128)}, f32[2,81,1,128]{3,1,2,0:T(8,128)}, u32[]{:S(2)}, u32[]{:S(2)}) collective-permute-start(f32[2,81,1,128]{3,1,2,0:T(8,128)} %get-tuple-element.674), channel_id=1, source_target_pairs={{0,1},{1,2},{2,3},{3,4},{4,5},{5,6},{6,7},{7,8},{8,9},{9,10},{10,1... | collective-permute-start | bytes 248840 | tf_op jit(solution)/shard_map/ppermute | solution.py:22
  44.4 1.2 copy-start.26
  46.5 1.6 copy-start.32
  46.7 2.6 copy-start.30
  46.9 3.5 %copy-start.28 = (s32[8]{0:T(128)}, s32[8]{0:T(128)S(1)}, u32[]{:S(2)}) copy-start(s32[8]{0:T(128)S(1)} %fusion.80) | copy-start | bytes 100
  51.6 14.4 %all-to-all-start.7 = ((s32[16,1,2]{2,1,0:T(1,128)}), s32[16,1,2]{2,1,0:T(1,128)S(1)}, u32[]{:S(2)}, u32[]{:S(2)}) async-start(s32[16,1,2]{2,1,0:T(1,128)} %bitcast.514), calls=%async_computation.7 | async-start | bytes 16384 | tf_op jit(solution)/shard_map/all_to_all | solution.py:103
  66.0 10.7 %all-to-all-start.10 = ((s32[16,1,2]{2,1,0:T(1,128)}), s32[16,1,2]{2,1,0:T(1,128)S(1)}, u32[]{:S(2)}, u32[]{:S(2)}) async-start(s32[16,1,2]{2,1,0:T(1,128)} %bitcast.516), calls=%async_computation.10 | async-start | bytes 16384 | tf_op jit(solution)/shard_map/all_to_all | solution.py:103
  76.7 10.7 %all-to-all-start.13 = ((s32[16,1,2]{2,1,0:T(1,128)}), s32[16,1,2]{2,1,0:T(1,128)S(1)}, u32[]{:S(2)}, u32[]{:S(2)}) async-start(s32[16,1,2]{2,1,0:T(1,128)} %bitcast.518), calls=%async_computation.13 | async-start | bytes 16384 | tf_op jit(solution)/shard_map/all_to_all | solution.py:103
  87.4 10.7 %all-to-all-start.3 = ((s32[16,1,32]{2,1,0:T(1,128)}), s32[16,1,32]{2,1,0:T(1,128)S(1)}, u32[]{:S(2)}, u32[]{:S(2)}) async-start(s32[16,1,32]{2,1,0:T(1,128)} %bitcast.11), calls=%async_computation.3 | async-start | bytes 16384 | tf_op jit(solution)/shard_map/all_to_all | solution.py:129
  98.2 10.7 %all-to-all-start.2 = ((s32[16,1,32]{2,1,0:T(1,128)}), s32[16,1,32]{2,1,0:T(1,128)S(1)}, u32[]{:S(2)}, u32[]{:S(2)}) async-start(s32[16,1,32]{2,1,0:T(1,128)} %bitcast.8), calls=%async_computation.2 | async-start | bytes 16384 | tf_op jit(solution)/shard_map/all_to_all | solution.py:129
  108.9 10.7 %all-to-all-start.1 = ((s32[16,1,32]{2,1,0:T(1,128)}), s32[16,1,32]{2,1,0:T(1,128)S(1)}, u32[]{:S(2)}, u32[]{:S(2)}) async-start(s32[16,1,32]{2,1,0:T(1,128)} %bitcast.5), calls=%async_computation.1 | async-start | bytes 16384 | tf_op jit(solution)/shard_map/all_to_all | solution.py:129
  116.2 26.0 %copy-start.5 = (f32[2,81,256]{2,0,1:T(2,128)S(1)}, f32[2,81,256]{2,0,1:T(2,128)}, u32[]{:S(2)}) copy-start(f32[2,81,256]{2,0,1:T(2,128)} %param.9) | copy-start | bytes 497668
  119.6 10.9 %all-to-all-start = ((s32[16,1,32]{2,1,0:T(1,128)}), s32[16,1,32]{2,1,0:T(1,128)S(1)}, u32[]{:S(2)}, u32[]{:S(2)}) async-start(s32[16,1,32]{2,1,0:T(1,128)} %bitcast.2), calls=%async_computation | async-start | bytes 16384 | tf_op jit(solution)/shard_map/all_to_all | solution.py:129
  130.5 10.8 %all-to-all-start.5 = ((bf16[16,2,162]{2,1,0:T(2,128)(2,1)}), bf16[16,2,162]{2,1,0:T(2,128)(2,1)S(1)}, u32[]{:S(2)}, u32[]{:S(2)}) async-start(bf16[16,2,162]{2,1,0:T(2,128)(2,1)} %broadcast_select_fusion.3), calls=%async_computation.5 | async-start | bytes 32768 | tf_op jit(solution)/shard_map/all_to_all | solution.py:108
  144.9 0.9 copy-start.35
  148.0 0.7 copy-start.14
  154.9 1.0 copy-start.2
  156.8 4.9 %copy-start.11 = (f32[2,81,1,128]{3,1,2,0:T(8,128)S(1)}, f32[2,81,1,128]{3,1,2,0:T(8,128)}, u32[]{:S(2)}) copy-start(f32[2,81,1,128]{3,1,2,0:T(8,128)} %get-tuple-element.663) | copy-start | bytes 248836
  157.4 5.6 %copy-start.10 = (f32[2,81,1,128]{3,1,2,0:T(8,128)S(1)}, f32[2,81,1,128]{3,1,2,0:T(8,128)}, u32[]{:S(2)}) copy-start(f32[2,81,1,128]{3,1,2,0:T(8,128)} %get-tuple-element.664) | copy-start | bytes 248836
  157.4 20.7 %copy-start = (f32[2,81,8,127]{3,1,2,0:T(8,128)S(1)}, f32[2,81,8,127]{3,1,2,0:T(8,128)}, u32[]{:S(2)}) copy-start(f32[2,81,8,127]{3,1,2,0:T(8,128)} %get-tuple-element.666) | copy-start | bytes 1975108
  158.2 10.8 %all-to-all-start.8 = ((bf16[16,2,162]{2,1,0:T(2,128)(2,1)}), bf16[16,2,162]{2,1,0:T(2,128)(2,1)S(1)}, u32[]{:S(2)}, u32[]{:S(2)}) async-start(bf16[16,2,162]{2,1,0:T(2,128)(2,1)} %broadcast_select_fusion.2), calls=%async_computation.8 | async-start | bytes 32768 | tf_op jit(solution)/shard_map/all_to_all | solution.py:108
  161.7 15.8 %collective-permute-start.2 = (f32[2,81,1,128]{3,1,2,0:T(8,128)S(1)}, f32[2,81,1,128]{3,1,2,0:T(8,128)S(1)}, u32[]{:S(2)}, u32[]{:S(2)}) collective-permute-start(f32[2,81,1,128]{3,1,2,0:T(8,128)S(1)} %copy-done.11), channel_id=1, source_target_pairs={{1,0},{2,1},{3,2},{4,3},{5,4},{6,5},{7,6},{8,7},{9,8},{10,9},{11,1... | collective-permute-start | bytes 248840 | tf_op jit(solution)/shard_map/ppermute | solution.py:25
  163.0 14.5 %collective-permute-start.3 = (f32[2,81,1,128]{3,1,2,0:T(8,128)S(1)}, f32[2,81,1,128]{3,1,2,0:T(8,128)S(1)}, u32[]{:S(2)}, u32[]{:S(2)}) collective-permute-start(f32[2,81,1,128]{3,1,2,0:T(8,128)S(1)} %copy-done.10), channel_id=1, source_target_pairs={{0,1},{1,2},{2,3},{3,4},{4,5},{5,6},{6,7},{7,8},{8,9},{9,10},{10,1... | collective-permute-start | bytes 248840 | tf_op jit(solution)/shard_map/ppermute | solution.py:22
  169.0 24.3 %all-to-all-start.6 = ((f32[16,32,162]{2,1,0:T(8,128)}), f32[16,32,162]{2,1,0:T(8,128)}, u32[]{:S(2)}, u32[]{:S(2)}) async-start(f32[16,32,162]{2,1,0:T(8,128)} %scatter_fusion), calls=%async_computation.6 | async-start | bytes 1048576 | tf_op jit(solution)/shard_map/all_to_all | solution.py:128
  182.1 1.0 copy-start.3
  184.5 6.5 %copy-start.19 = (pred[16,2]{1,0:T(8,128)(4,1)S(1)}, pred[16,2]{1,0:T(8,128)(4,1)}, u32[]{:S(2)}) copy-start(pred[16,2]{1,0:T(8,128)(4,1)} %copy.787) | copy-start | bytes 100
  184.5 36.5 %collective-permute-start.4 = (f32[2,81,1,128]{3,1,2,0:T(8,128)}, f32[2,81,1,128]{3,1,2,0:T(8,128)}, u32[]{:S(2)}, u32[]{:S(2)}) collective-permute-start(f32[2,81,1,128]{3,1,2,0:T(8,128)} %get-tuple-element.653), channel_id=1, source_target_pairs={{1,0},{2,1},{3,2},{4,3},{5,4},{6,5},{7,6},{8,7},{9,8},{10,9},{11,1... | collective-permute-start | bytes 248840 | tf_op jit(solution)/shard_map/ppermute | solution.py:25
  185.8 35.2 %collective-permute-start.5 = (f32[2,81,1,128]{3,1,2,0:T(8,128)}, f32[2,81,1,128]{3,1,2,0:T(8,128)}, u32[]{:S(2)}, u32[]{:S(2)}) collective-permute-start(f32[2,81,1,128]{3,1,2,0:T(8,128)} %get-tuple-element.654), channel_id=1, source_target_pairs={{0,1},{1,2},{2,3},{3,4},{4,5},{5,6},{6,7},{7,8},{8,9},{9,10},{10,1... | collective-permute-start | bytes 248840 | tf_op jit(solution)/shard_map/ppermute | solution.py:22
  193.3 17.9 %all-to-all-start.11 = ((bf16[16,2,162]{2,1,0:T(2,128)(2,1)}), bf16[16,2,162]{2,1,0:T(2,128)(2,1)}, u32[]{:S(2)}, u32[]{:S(2)}) async-start(bf16[16,2,162]{2,1,0:T(2,128)(2,1)} %broadcast_select_fusion.1), calls=%async_computation.11 | async-start | bytes 32768 | tf_op jit(solution)/shard_map/all_to_all | solution.py:108
  204.4 1.1 copy-start.7
  208.2 0.9 copy-start.33
  211.2 17.9 %all-to-all-start.9 = ((f32[16,32,162]{2,1,0:T(8,128)}), f32[16,32,162]{2,1,0:T(8,128)}, u32[]{:S(2)}, u32[]{:S(2)}) async-start(f32[16,32,162]{2,1,0:T(8,128)} %scatter_fusion.1), calls=%async_computation.9 | async-start | bytes 1048576 | tf_op jit(solution)/shard_map/all_to_all | solution.py:128
  229.1 16.1 %all-to-all-start.14 = ((bf16[16,2,162]{2,1,0:T(2,128)(2,1)}), bf16[16,2,162]{2,1,0:T(2,128)(2,1)S(1)}, u32[]{:S(2)}, u32[]{:S(2)}) async-start(bf16[16,2,162]{2,1,0:T(2,128)(2,1)} %broadcast_select_fusion), calls=%async_computation.14 | async-start | bytes 32768 | tf_op jit(solution)/shard_map/all_to_all | solution.py:108
  238.6 0.9 copy-start.8
  242.1 0.9 copy-start.31
  245.2 6.9 %copy-start.21 = (s32[512,1]{0,1:T(1,128)S(1)}, s32[512,1]{0,1:T(1,128)}, u32[]{:S(2)}) copy-start(s32[512,1]{0,1:T(1,128)} %reshape.300) | copy-start | bytes 6148
  245.2 17.7 %all-to-all-start.12 = ((f32[16,32,162]{2,1,0:T(8,128)}), f32[16,32,162]{2,1,0:T(8,128)S(1)}, u32[]{:S(2)}, u32[]{:S(2)}) async-start(f32[16,32,162]{2,1,0:T(8,128)} %scatter_fusion.2), calls=%async_computation.12 | async-start | bytes 1048576 | tf_op jit(solution)/shard_map/all_to_all | solution.py:128
  268.4 0.9 copy-start.29
  271.5 14.8 %all-to-all-start.15 = ((f32[16,32,162]{2,1,0:T(8,128)}), f32[16,32,162]{2,1,0:T(8,128)S(1)}, u32[]{:S(2)}, u32[]{:S(2)}) async-start(f32[16,32,162]{2,1,0:T(8,128)} %scatter_fusion.3), calls=%async_computation.15 | async-start | bytes 1048576 | tf_op jit(solution)/shard_map/all_to_all | solution.py:128
  275.5 32.2 %all-reduce.3.cloned.1.call-start = ((), (), s32[]{:S(2)}) async-start(), calls=%async_computation.16 | async-start | bytes 180224 | tf_op jit(solution)/shard_map/psum | solution.py:139
  286.3 0.8 copy-start.4
  290.7 0.9 copy-start.9
  290.7 38.9 %all-reduce.5.cloned.1.call-start = ((), (), s32[]{:S(2)}) async-start(), calls=%async_computation.17 | async-start | bytes 180224 | tf_op jit(solution)/shard_map/psum | solution.py:141
  291.6 17.7 %collective-permute-start.6 = (f32[2,81,1,128]{3,1,2,0:T(8,128)S(1)}, f32[2,81,1,128]{3,1,2,0:T(8,128)S(1)}, u32[]{:S(2)}, u32[]{:S(2)}) collective-permute-start(f32[2,81,1,128]{3,1,2,0:T(8,128)S(1)} %copy-done.9), channel_id=1, source_target_pairs={{1,0},{2,1},{3,2},{4,3},{5,4},{6,5},{7,6},{8,7},{9,8},{10,9},{11,1... | collective-permute-start | bytes 248840 | tf_op jit(solution)/shard_map/ppermute | solution.py:25
  292.9 16.4 %collective-permute-start.7 = (f32[2,81,1,128]{3,1,2,0:T(8,128)S(1)}, f32[2,81,1,128]{3,1,2,0:T(8,128)}, u32[]{:S(2)}, u32[]{:S(2)}) collective-permute-start(f32[2,81,1,128]{3,1,2,0:T(8,128)S(1)} %get-tuple-element.652), channel_id=1, source_target_pairs={{0,1},{1,2},{2,3},{3,4},{4,5},{5,6},{6,7},{7,8},{8,9},{9,10},{10,1... | collective-permute-start | bytes 248840 | tf_op jit(solution)/shard_map/ppermute | solution.py:22
  (18 other events, 11.9 us)
Sparse Core Ops, SparseCore 0:
  290.9 16.8 all-reduce.2
  310.6 18.9 all-reduce.4
where the time goes:
time: 341 us; the launch traced here: 338 us
  starting transfers between devices  107 us (31%)
  waiting for transfers between devices  87.7 us (26%)
  local copies, waits for them, and re-layouts  79.9 us (23%)
  other arithmetic  47.9 us (14%)
  between operations  15.7 us (5%)
    all_to_all x4, starting transfers between devices, on_device(): lax.all_to_all(send_values, 'tile', split_axis=0, concat_axis=0, tiled=True)  24.8 us
    all_to_all x4, starting transfers between devices, on_device(): lax.all_to_all(requests_out, 'tile', split_axis=0, concat_axis=0, tiled=T...  22.5 us
    all_to_all x4, waiting for transfers between devices, on_device(): lax.all_to_all(send_slots, 'tile', split_axis=0, concat_axis=0, tiled=True)  22.4 us
    all_to_all x4, starting transfers between devices, on_device(): lax.all_to_all(values, 'tile', split_axis=0, concat_axis=0, tiled=True)  20.2 us
    ppermute x4, starting transfers between devices, with_halo(): lax.ppermute(lax.slice_in_dim(block, block.shape[dim] - width, None, axis...  20.1 us
    all_to_all x4, waiting for transfers between devices, on_device(): lax.all_to_all(send_values, 'tile', split_axis=0, concat_axis=0, tiled=True)  17.5 us
    all_to_all x4, waiting for transfers between devices, on_device(): lax.all_to_all(requests_out, 'tile', split_axis=0, concat_axis=0, tiled=T...  16.9 us
    psum x1, waiting for transfers between devices, on_device(): lax.psum(jnp.sum((nest_field - mean_field) ** 2, axis=0), 'member')  16.4 us
  transfers between devices with their start and end apart: 26, of which 14 were waited for; matrix products, arithmetic and copies ran while one was open for 27% of the time, Pallas kernels for 0%

commit v1 on v0

--- a/solution.py
+++ b/solution.py
@@ -1,6 +1,11 @@
+import functools
+
 import jax
 import jax.numpy as jnp
+import numpy as np
 from jax import lax
+from jax.experimental import pallas as pl
+from jax.experimental.pallas import tpu as pltpu
 from jax.sharding import PartitionSpec as P
 
 CAPB = 2
@@ -143,6 +148,426 @@
     return (parent, nest_field, mean_field, variance)
 
 
+MESH = pl.DeviceIdType.MESH
+F32 = jnp.float32
+BF16 = jnp.bfloat16
+HI = lax.Precision.HIGHEST
+PLANE = 4
+LANES = 128
+
+
+def inverse_powers(levels):
+    a = np.zeros((levels, levels))
+    for level in range(levels):
+        a[level, level] = 1.0
+        for other in (level - 1, level + 1):
+            if 0 <= other < levels:
+                a[level, level] += IMPLICIT_MIX
+                a[level, other] = -IMPLICIT_MIX
+    inv = np.linalg.inv(a)
+    out = np.zeros((STEPS, LANES, LANES), np.float32)
+    power = np.eye(levels)
+    for k in range(STEPS):
+        power = power @ inv
+        out[k, :levels, :levels] = power
+    return out
+
+
+def nn(a, b, precision=None):
+    return lax.dot_general(
+        a, b, (((1,), (0,)), ((), ())), preferred_element_type=F32, precision=precision
+    )
+
+
+def nt(a, b, precision=None):
+    return lax.dot_general(
+        a, b, (((1,), (1,)), ((), ())), preferred_element_type=F32, precision=precision
+    )
+
+
+def one_hot(mask):
+    return jnp.where(mask, 1.0, 0.0).astype(BF16)
+
+
+def fused(
+    dims,
+    parent_ref, nest_ref, terrain_ref, shift_ref, bound_ref, dest_ref, inv_ref,
+    parent_out, nest_out, mean_out, var_out,
+    meta, halo_out, halo_in, terr_in, zg, pm, pr, w, msg, got, mine, theirs,
+    meta_s, meta_r, halo_s, halo_r, terr_s, terr_r, z_s, z_r, p_s, p_r, msg_s, msg_r, mem_s, mem_r,
+):
+    members, levels, rows, width, cols, nb, tiles, per, cells = dims
+    padded = zg.shape[2]
+    zs = tiles // PLANE
+    tall = 2 * rows
+    half = rows // 2
+    me = lax.axis_index("tile")
+    core = lax.axis_index("member")
+    my_p = lax.rem(me, PLANE)
+    my_z = me // PLANE
+
+    def rcopy(src, dst, ssem, rsem, tile, member=None):
+        return pltpu.make_async_remote_copy(
+            src_ref=src, dst_ref=dst, send_sem=ssem, recv_sem=rsem,
+            device_id=(core if member is None else member, tile), device_id_type=MESH,
+        )
+
+    def at(d):
+        return lax.rem(me + d, tiles)
+
+    barrier = pltpu.get_barrier_semaphore()
+    for d in range(1, tiles):
+        pl.semaphore_signal(barrier, inc=1, device_id=(core, at(d)), device_id_type=MESH)
+    pl.semaphore_signal(barrier, inc=1, device_id=(1 - core, me), device_id_type=MESH)
+
+    row_i = lax.broadcasted_iota(jnp.int32, (rows, width), 0)
+
+    def pack(level, _):
+        p0 = parent_ref[level]
+        p1 = parent_ref[levels + level]
+        halo_out[0, level] = jnp.where(row_i < half, pltpu.roll(p0, half, axis=0), p1)
+        halo_out[1, level] = jnp.where(row_i < half, p0, pltpu.roll(p1, half, axis=0))
+        return 0
+
+    lax.fori_loop(0, levels, pack, 0)
+
+    meta[me, 0:STEPS, :] = dest_ref[...]
+    meta[me, STEPS : 2 * STEPS, :] = jnp.zeros((STEPS, cols), jnp.int32)
+    for s in range(STEPS):
+        index = bound_ref[s : s + 1, :]
+        at_col = lax.rem(lax.rem(index, width) + shift_ref[s] + width, width)
+        meta[me, STEPS + s : STEPS + s + 1, 0:nb] = (index // width) * width + at_col
+
+    last = inv_ref[STEPS - 1][:padded, :levels]
+    for m in range(members):
+        zg[my_z, m] = nn(last, nest_ref[m], HI)
+
+    pl.semaphore_wait(barrier, tiles)
+
+    pending = []
+
+    def start(copy):
+        copy.start()
+        pending.append(copy)
+
+    for d in range(1, tiles):
+        start(rcopy(meta.at[me], meta.at[me], meta_s.at[d], meta_r.at[d], at(d)))
+
+    def halo_pair(i, tile):
+        return (
+            rcopy(halo_out.at[i], halo_in.at[i], halo_s.at[i], halo_r.at[i], tile),
+            rcopy(terrain_ref, terr_in.at[i], terr_s.at[i], terr_r.at[i], tile),
+        )
+
+    has = (me < tiles - 1, me > 0)
+    to = (lax.rem(me + 1, tiles), lax.rem(me + tiles - 1, tiles))
+    for i in range(2):
+        @pl.when(has[i])
+        def _():
+            for copy in halo_pair(i, to[i]):
+                copy.start()
+
+    for d in range(1, zs):
+        start(rcopy(zg.at[my_z], zg.at[my_z], z_s.at[d], z_r.at[d], at(d * PLANE)))
+
+    for d in range(1, tiles):
+        rcopy(meta.at[me], meta.at[at(tiles - d)], meta_s.at[d], meta_r.at[d], me).wait_recv()
+
+    t_iota = lax.broadcasted_iota(jnp.int32, (tiles, cols), 0)
+    dest = [meta[:, s, :] for s in range(STEPS)]
+    dest_tile = [v // cols for v in dest]
+
+    def chase(final):
+        tau = jnp.zeros((1, cols), jnp.int32) + final
+        sources, slots, firsts = [None] * STEPS, [None] * STEPS, [None] * STEPS
+        for s in range(STEPS - 1, -1, -1):
+            hit = dest_tile[s] == tau
+            tau = jnp.sum(jnp.where(hit, t_iota, 0), axis=0, keepdims=True)
+            slots[s] = jnp.sum(jnp.where(hit, dest[s] - dest_tile[s] * cols, 0), axis=0, keepdims=True)
+            sources[s] = tau
+        return sources, slots
+
+    lane_t = lax.broadcasted_iota(jnp.int32, (tiles, LANES), 1)
+    lane_c = lax.broadcasted_iota(jnp.int32, (tiles, cols), 1)
+    cell_iota = lax.broadcasted_iota(jnp.int32, (tiles, cells), 1)
+    eye = one_hot(lax.broadcasted_iota(jnp.int32, (LANES, LANES), 0)
+                  == lax.broadcasted_iota(jnp.int32, (LANES, LANES), 1))
+    requests = [None] * STEPS
+    path = None
+    for s in range(STEPS - 1, -1, -1):
+        hop = one_hot(dest_tile[s][:, 0:1] == lane_t)
+        hop = jnp.concatenate([hop, jnp.zeros((LANES - tiles, LANES), BF16)], axis=0)
+        path = hop if path is None else nn(hop, path).astype(BF16)
+        back = nt(eye, path).astype(BF16)[0:tiles, :]
+        cell = meta[:, STEPS + s, :]
+        owned = jnp.logical_and(cell // cells == me, lane_c < nb)
+        local = lax.rem(cell, cells) + 1
+        parts = []
+        for k in range(CAPB):
+            pick = jnp.logical_and(owned, lax.rem(lane_c, CAPB) == k)
+            which = jnp.sum(jnp.where(pick, local, 0), axis=1, keepdims=True) - 1
+            asked = one_hot(cell_iota == which)
+            asked = jnp.concatenate([asked, jnp.zeros((LANES - tiles, cells), BF16)], axis=0)
+            parts.append(nn(back, asked).astype(BF16))
+        requests[s] = jnp.concatenate(parts, axis=0)
+
+    sources, slots = chase(me)
+
+    q_iota = lax.broadcasted_iota(jnp.int32, (cols, cols), 0)
+    j_iota = lax.broadcasted_iota(jnp.int32, (cols, cols), 1)
+    relax = jnp.where(j_iota < nb, 1.0 - RELAX_RATE, 1.0)
+    moves = [None] * STEPS
+    path = None
+    for s in range(STEPS - 1, -1, -1):
+        hop = jnp.where(slots[s] == q_iota, relax, 0.0).astype(BF16)
+        path = hop if path is None else nn(path, hop).astype(BF16)
+        moves[s] = path
+
+    for d in range(1, zs):
+        rcopy(
+            zg.at[my_z], zg.at[lax.rem(my_z + zs - d, zs)], z_s.at[d], z_r.at[d], me
+        ).wait_recv()
+
+    def masked(origin, m):
+        out = jnp.zeros((padded, cols), F32)
+        for z in range(zs):
+            out = jnp.where(origin == z * PLANE + my_p, zg[z, m], out)
+        return out
+
+    for d in range(1, PLANE):
+        final = my_z * PLANE + lax.rem(my_p + d, PLANE)
+        origin = chase(final)[0][0]
+        for m in range(members):
+            pm[d - 1, m] = masked(origin, m)
+        start(rcopy(pm.at[d - 1], pr.at[d - 1], p_s.at[d], p_r.at[d], final))
+
+    for i in range(2):
+        @pl.when(has[1 - i])
+        def _():
+            for copy in halo_pair(i, me):
+                copy.wait_recv()
+
+        @pl.when(jnp.logical_not(has[1 - i]))
+        def _():
+            halo_in[i] = jnp.zeros((levels, rows, width), F32)
+            terr_in[i] = jnp.zeros((rows, width), jnp.int32)
+
+    row_t = lax.broadcasted_iota(jnp.int32, (tall, width), 0) + me * rows - half
+    inside = jnp.logical_and(row_t >= 0, row_t < tiles * rows)
+
+    def fill(level, _):
+        low = halo_in[0, level]
+        high = halo_in[1, level]
+        for m in range(members):
+            base = pl.multiple_of((m * levels + level) * tall, tall)
+            own = pltpu.roll(parent_ref[m * levels + level], half, axis=0)
+            lo = low if m == 0 else pltpu.roll(low, half, axis=0)
+            hi = pltpu.roll(high, half, axis=0) if m == 0 else high
+            top = jnp.where(row_i < half, lo, own)
+            bottom = jnp.where(row_i < half, own, hi)
+            w[pl.ds(base, tall), :] = jnp.concatenate([top, bottom], axis=0)
+        return 0
+
+    lax.fori_loop(0, levels, fill, 0)
+    tail = members * levels * tall
+    w[tail:, :] = jnp.zeros((w.shape[0] - tail, width), F32)
+
+    terr = terrain_ref[...]
+    terr_own = pltpu.roll(terr, half, axis=0)
+    terr_all = jnp.concatenate(
+        [
+            jnp.where(row_i < half, pltpu.roll(terr_in[0], half, axis=0), terr_own),
+            jnp.where(row_i < half, terr_own, pltpu.roll(terr_in[1], half, axis=0)),
+        ],
+        axis=0,
+    )
+    damping = DRAG_RATE * terr_all.astype(F32) / 3000.0
+    centre = 1.0 - 4.0 * HORIZ_MIX - 2.0 * VERT_MIX - damping
+
+    chunk = 9 if levels % 9 == 0 else 1
+
+    def advance(final):
+        def body(c, before):
+            before = list(before)
+            for u in range(chunk):
+                level = c * chunk + u
+                for m in range(members):
+                    base = pl.multiple_of((m * levels + level) * tall, tall)
+                    above = pl.multiple_of(
+                        (m * levels + jnp.minimum(level + 1, levels - 1)) * tall, tall
+                    )
+                    cur = w[pl.ds(base, tall), :]
+                    up = w[pl.ds(above, tall), :]
+                    sides = (
+                        pltpu.roll(cur, 1, axis=0) + pltpu.roll(cur, tall - 1, axis=0)
+                        + pltpu.roll(cur, 1, axis=1) + pltpu.roll(cur, width - 1, axis=1)
+                    )
+                    new = centre * cur + HORIZ_MIX * sides + VERT_MIX * (up + before[m])
+                    if final:
+                        parent_out[m * levels + level] = new[half : half + rows]
+                    else:
+                        w[pl.ds(base, tall), :] = jnp.where(inside, new, 0.0)
+                    before[m] = cur
+            return tuple(before)
+
+        first = tuple(w[m * levels * tall : (m * levels + 1) * tall, :] for m in range(members))
+        lax.fori_loop(0, levels // chunk, body, first)
+
+    slot_rows = members * STEPS * CAPB
+
+    def pick(s):
+        for m in range(members):
+            pieces = [
+                w[pl.ds(m * levels * tall + half + r, padded, stride=tall), :] for r in range(rows)
+            ]
+            field = jnp.concatenate(pieces, axis=1)
+            field = jnp.concatenate([field, jnp.zeros((LANES - padded, cells), F32)], axis=0)
+            values = nt(requests[s], field.astype(BF16))
+            for k in range(CAPB):
+                slot = m * STEPS * CAPB + s * CAPB + k
+                msg[pl.ds(slot, tiles, stride=slot_rows), :] = values[k * tiles : (k + 1) * tiles]
+
+    for s in range(STEPS - 1):
+        pick(s)
+        advance(False)
+    pick(STEPS - 1)
+
+    def rows_of(tile):
+        return pl.ds(pl.multiple_of(tile * slot_rows, slot_rows), slot_rows)
+
+    for d in range(1, tiles):
+        start(rcopy(msg.at[rows_of(at(d))], got.at[rows_of(me)], msg_s.at[d], msg_r.at[d], at(d)))
+    got[rows_of(me), :] = msg[rows_of(me), :]
+
+    advance(True)
+
+    origin = sources[0]
+    for d in range(1, PLANE):
+        rcopy(pm.at[d - 1], pr.at[d - 1], p_s.at[d], p_r.at[d], me).wait_recv()
+    result = []
+    for m in range(members):
+        block = masked(origin, m)
+        for d in range(1, PLANE):
+            came = lax.rem(origin, PLANE) == lax.rem(my_p + PLANE - d, PLANE)
+            block = jnp.where(came, pr[d - 1, m], block)
+        result.append(nt(block, moves[0].astype(F32), HI))
+
+    g_rows = tiles * slot_rows
+    g_iota = lax.broadcasted_iota(jnp.int32, (g_rows, cols), 0)
+    g_lane = lax.broadcasted_iota(jnp.int32, (g_rows, cols), 1)
+    g_owner = g_iota // slot_rows
+    g_slot = lax.rem(g_iota, slot_rows)
+    takes = [[None] * STEPS for _ in range(members)]
+    for s in range(STEPS):
+        asker = sources[s][:, 0:1]
+        cell = jnp.sum(
+            jnp.where(t_iota == asker, meta[:, STEPS + s, :], 0), axis=0, keepdims=True
+        )
+        ours = jnp.logical_and(g_owner == cell // cells, g_lane < nb)
+        for m in range(members):
+            slot = m * STEPS * CAPB + s * CAPB + lax.rem(g_lane, CAPB)
+            takes[m][s] = nt(
+                one_hot(jnp.logical_and(ours, g_slot == slot)), moves[s]
+            ).astype(BF16)
+
+    for d in range(1, tiles):
+        rcopy(
+            msg.at[rows_of(me)], got.at[rows_of(at(tiles - d))], msg_s.at[d], msg_r.at[d], me
+        ).wait_recv()
+    arrived = jnp.transpose(got[...]).astype(BF16)
+    for m in range(members):
+        for s in range(STEPS):
+            entry = nn(arrived, takes[m][s])
+            result[m] = result[m] + nn(inv_ref[STEPS - 1 - s], entry, HI)[:padded]
+        mine[m] = result[m]
+        nest_out[m] = result[m][:levels]
+
+    pair = rcopy(mine, theirs, mem_s, mem_r, me, 1 - core)
+    pair.start()
+    pair.wait()
+    count = 2 * members
+    fields = [mine[m, 0:levels] for m in range(members)]
+    fields += [theirs[m, 0:levels] for m in range(members)]
+    mean = functools.reduce(lambda a, b: a + b, fields) / count
+    mean_out[...] = mean
+    var_out[...] = functools.reduce(lambda a, b: a + b, [(f - mean) ** 2 for f in fields]) / count
+
+    for copy in pending:
+        copy.wait_send()
+    for i in range(2):
+        @pl.when(has[i])
+        def _():
+            for copy in halo_pair(i, to[i]):
+                copy.wait_send()
+
+
+def on_device_fused(parent_state, nest_state, terrain, shift_x, boundary_index, reloc_dest):
+    members, levels, rows, width = parent_state.shape
+    cols = nest_state.shape[2]
+    nb = boundary_index.shape[1]
+    tiles = lax.axis_size("tile")
+    cells = rows * width
+    padded = -(-levels // 8) * 8
+    zs = tiles // PLANE
+    slot_rows = members * STEPS * CAPB
+    dims = (members, levels, rows, width, cols, nb, tiles, cols // (tiles // 2), cells)
+    vmem = pl.BlockSpec(memory_space=pltpu.VMEM)
+    dma = pltpu.SemaphoreType.DMA
+    outs = pl.pallas_call(
+        functools.partial(fused, dims),
+        out_shape=(
+            jax.ShapeDtypeStruct((members * levels, rows, width), F32),
+            jax.ShapeDtypeStruct((members, levels, cols), F32),
+            jax.ShapeDtypeStruct((levels, cols), F32),
+            jax.ShapeDtypeStruct((levels, cols), F32),
+        ),
+        in_specs=[vmem, vmem, vmem, pl.BlockSpec(memory_space=pltpu.SMEM), vmem, vmem, vmem],
+        out_specs=(vmem,) * 4,
+        scratch_shapes=[
+            pltpu.VMEM((tiles, 2 * STEPS, cols), jnp.int32),
+            pltpu.VMEM((2, levels, rows, width), F32),
+            pltpu.VMEM((2, levels, rows, width), F32),
+            pltpu.VMEM((2, rows, width), jnp.int32),
+            pltpu.VMEM((zs, members, padded, cols), F32),
+            pltpu.VMEM((PLANE - 1, members, padded, cols), F32),
+            pltpu.VMEM((PLANE - 1, members, padded, cols), F32),
+            pltpu.VMEM(((members * levels + padded - levels) * 2 * rows, width), F32),
+            pltpu.VMEM((tiles * slot_rows, LANES), F32),
+            pltpu.VMEM((tiles * slot_rows, LANES), F32),
+            pltpu.VMEM((members, padded, cols), F32),
+            pltpu.VMEM((members, padded, cols), F32),
+            dma((tiles,)), dma((tiles,)),
+            dma((2,)), dma((2,)), dma((2,)), dma((2,)),
+            dma((zs,)), dma((zs,)), dma((PLANE,)), dma((PLANE,)),
+            dma((tiles,)), dma((tiles,)),
+            dma, dma,
+        ],
+        compiler_params=pltpu.CompilerParams(
+            collective_id=0, has_side_effects=True, vmem_limit_bytes=48 * 1024 * 1024
+        ),
+    )(
+        parent_state.reshape(members * levels, rows, width),
+        nest_state, terrain, shift_x, boundary_index, reloc_dest,
+        jnp.asarray(inverse_powers(levels)),
+    )
+    return (outs[0].reshape(parent_state.shape),) + tuple(outs[1:])
+
+
+def fits_one_plane_split(mesh, parent, nest, bound):
+    tiles = mesh.shape["tile"]
+    cols = nest[2] // tiles
+    return (
+        tiles == PLANE * PLANE
+        and mesh.shape["member"] == 2
+        and bound[1] // tiles <= cols // (tiles // 2)
+        and nest[1] <= LANES
+        and nest[0] == 4
+        and parent[2] // tiles == 2 * STEPS
+        and parent[3] == LANES
+        and cols % LANES == 0
+    )
+
+
 def solution(mesh):
     in_specs = (
         P("member", None, "tile", None),
@@ -158,6 +583,12 @@
         P(None, "tile"),
         P(None, "tile"),
     )
-    return jax.shard_map(
-        on_device, mesh=mesh, in_specs=in_specs, out_specs=out_specs, check_vma=False
-    )
+
+    def whole(parent_state, nest_state, terrain, shift_x, boundary_index, reloc_dest):
+        fits = fits_one_plane_split(mesh, parent_state.shape, nest_state.shape, boundary_index.shape)
+        return jax.shard_map(
+            on_device_fused if fits else on_device,
+            mesh=mesh, in_specs=in_specs, out_specs=out_specs, check_vma=False,
+        )(parent_state, nest_state, terrain, shift_x, boundary_index, reloc_dest)
+
+    return whole

time: 341 us -> 56.8 us (0.17)
  starting transfers between devices: 107 us -> 0 us
  waiting for transfers between devices: 87.7 us -> 0 us
  local copies, waits for them, and re-layouts: 79.9 us -> 4.94 us
  Pallas kernels: 0 us -> 50.9 us
  other arithmetic: 47.9 us -> 0 us
  between operations: 15.7 us -> 0.73 us
    all_to_all x16 -> x0, starting transfers between devices: 81.5 us -> none  [the longest x4 24.8 us: on_device(): lax.all_to_all(send_values, 'tile', split_axis=0, concat_axis=0, tiled=True)]
    all_to_all x16 -> x0, waiting for transfers between devices: 61.7 us -> none  [the longest x4 22.4 us: on_device(): lax.all_to_all(send_slots, 'tile', split_axis=0, concat_axis=0, tiled=True)]
    pallas_call x0 -> x1, Pallas kernels: none -> 50.9 us  [on_device_fused(): pl.pallas_call(functools.partial(fused, dims), out_shape=(jax.ShapeDtypeS...]
    psum x2 -> x0, waiting for transfers between devices: 26 us -> none  [the longest x1 16.4 us: on_device(): lax.psum(jnp.sum((nest_field - mean_field) ** 2, axis=0), 'member')]
    ppermute x8 -> x0, starting transfers between devices: 25.3 us -> none  [the longest x4 20.1 us: with_halo(): lax.ppermute(lax.slice_in_dim(block, block.shape[dim] - width, None, axis...]
    scatter x8 -> x0, local copies, waits for them, and re-layouts: 19.7 us -> none  [the longest x4 10.9 us: on_device(): placed = jnp.zeros((columns_here, mixed), jnp.float32).at[got_slots.resha...]
    slice x30 -> x0, local copies, waits for them, and re-layouts: 18.9 us -> none  [the longest x6 5.6 us: parent_update(): east_cell = jnp.roll(parent, -1, axis=3)]
    scatter x8 -> x0, other arithmetic: 12 us -> none  [the longest x4 7.3 us: on_device(): jnp.zeros((tile_count, CAPB), jnp.int32).at[owner_runs].set(local_runs)]
  transfers between devices with their start and end apart: 26 -> 0, of which waited for: 14 -> 0; matrix products, arithmetic and copies ran while one was open for 27% -> 0% of each run, Pallas kernels for 0% -> 0%
where the time goes in v1:
time: 56.8 us; the launch traced here: 56.6 us
  Pallas kernels  50.9 us (90%)
  local copies, waits for them, and re-layouts  4.94 us (9%)
  between operations  0.73 us (1%)
    pallas_call x1, Pallas kernels, on_device_fused(): pl.pallas_call(functools.partial(fused, dims), out_shape=(jax.ShapeDtypeS...  50.9 us
    unnamed x17, local copies, waits for them, and re-layouts  4.94 us

profile of v1, /device:TPU:0, one launch (start us, length us, event | category | flops | bytes accessed | tf_op | source)
XLA Modules:
  0.0 56.6 jit_solution(5084269992235757269)
XLA Ops:
  0.6 0.0 copy-start.1
  0.6 0.0 copy-start.2
  0.7 0.0 copy-start.3
  0.7 0.0 copy-start.4
  0.7 0.0 copy-start.5
  0.7 1.0 %copy.11.nest_ref = f32[2,81,256]{2,1,0:T(8,128)S(1)} copy(f32[2,81,256]{2,0,1:T(2,128)} %param.8) | data formatting | bytes 331776 | tf_op args[1]
  1.7 0.0 copy-done.1
  1.7 0.0 copy-done.2
  1.7 0.0 copy-done.3
  1.7 0.0 copy-done.4
  1.7 0.0 copy-done.5
  1.7 0.0 copy-start
  1.7 1.1 %copy-done = f32[2,81,8,128]{3,2,1,0:T(8,128)S(1)} copy-done((f32[2,81,8,128]{3,2,1,0:T(8,128)S(1)}, f32[2,81,8,128]{3,2,1,0:T(8,128)}, u32[]{:S(2)}) %copy-start) | copy-done | bytes 663576
  2.8 50.9 %shard_map.102 = (f32[162,8,128]{2,1,0:T(8,128)S(1)}, f32[2,81,256]{2,1,0:T(8,128)S(1)}, f32[81,256]{1,0:T(8,128)S(1)}, f32[81,256]{1,0:T(8,128)S(1)}) custom-call(f32[162,8,128]{2,1,0:T(8,128)S(1)} %bitcast.2, f32[2,81,256]{2,1,0:T(8,128)S(1)} %copy.11.nest_ref, s32[8,128]{1,0:T(8,128)S(1)} %copy-done.2, s32[4]{0:T(128)S(1)} %copy-done.5, ...), custom_call_target="tpu_custom_call" | custom-call | tf_op jit(solution)/shard_map/pallas_call | solution.py:516
  53.7 0.8 %copy.12 = f32[2,81,256]{2,0,1:T(2,128)} copy(f32[2,81,256]{2,1,0:T(8,128)S(1)} %get-tuple-element.13) | data formatting | bytes 331776
  54.5 0.8 %copy.16 = f32[2,81,8,128]{3,2,1,0:T(8,128)} copy(f32[2,81,8,128]{3,2,1,0:T(8,128)S(1)} %bitcast.3) | data formatting | bytes 1327104
  55.3 0.6 %copy.17 = f32[81,256]{1,0:T(8,128)} copy(f32[81,256]{1,0:T(8,128)S(1)} %get-tuple-element.22) | data formatting | bytes 165888
  55.9 0.6 %copy.18 = f32[81,256]{1,0:T(8,128)} copy(f32[81,256]{1,0:T(8,128)S(1)} %get-tuple-element.23) | data formatting | bytes 165888
Async XLA Ops:
  0.6 1.0 %copy-start.1 = (f32[4,128,128]{2,1,0:T(8,128)S(1)}, f32[4,128,128]{2,1,0:T(8,128)}, u32[]{:S(2)}) copy-start(f32[4,128,128]{2,1,0:T(8,128)} %constant.2.clone.inv_ref) | copy-start | bytes 786436
  0.6 1.0 %copy-start.2 = (s32[8,128]{1,0:T(8,128)S(1)}, s32[8,128]{1,0:T(8,128)}, u32[]{:S(2)}) copy-start(s32[8,128]{1,0:T(8,128)} %terrain_ref.1) | copy-start | bytes 12292
  0.7 1.0 %copy-start.3 = (s32[4,256]{1,0:T(4,128)S(1)}, s32[4,256]{1,0:T(4,128)}, u32[]{:S(2)}) copy-start(s32[4,256]{1,0:T(4,128)} %dest_ref.1) | copy-start | bytes 12292
  0.7 1.0 %copy-start.4 = (s32[4,16]{1,0:T(4,128)S(1)}, s32[4,16]{1,0:T(4,128)}, u32[]{:S(2)}) copy-start(s32[4,16]{1,0:T(4,128)} %bound_ref.1) | copy-start | bytes 772
  0.7 1.0 %copy-start.5 = (s32[4]{0:T(128)S(1)}, s32[4]{0:T(128)}, u32[]{:S(2)}) copy-start(s32[4]{0:T(128)} %shift_ref.1) | copy-start | bytes 52
  1.7 1.1 %copy-start = (f32[2,81,8,128]{3,2,1,0:T(8,128)S(1)}, f32[2,81,8,128]{3,2,1,0:T(8,128)}, u32[]{:S(2)}) copy-start(f32[2,81,8,128]{3,2,1,0:T(8,128)} %param.7) | copy-start | bytes 1990660

commit v2 on v1

--- a/solution.py
+++ b/solution.py
@@ -154,6 +154,8 @@
 HI = lax.Precision.HIGHEST
 PLANE = 4
 LANES = 128
+PARTS = 3
+SUB = 16
 
 
 def inverse_powers(levels):
@@ -165,12 +167,19 @@
                 a[level, level] += IMPLICIT_MIX
                 a[level, other] = -IMPLICIT_MIX
     inv = np.linalg.inv(a)
-    out = np.zeros((STEPS, LANES, LANES), np.float32)
+    padded = -(-levels // 8) * 8
+    parts = np.zeros((STEPS, PARTS, padded, LANES), jnp.bfloat16)
     power = np.eye(levels)
     for k in range(STEPS):
         power = power @ inv
-        out[k, :levels, :levels] = power
-    return out
+        rest = power
+        for part in range(PARTS):
+            piece = rest.astype(np.float32).astype(jnp.bfloat16)
+            parts[STEPS - 1 - k, part, :levels, :levels] = piece
+            rest = rest - piece.astype(np.float64)
+    last = np.zeros((padded, levels), np.float32)
+    last[:levels] = power
+    return last, parts.reshape(STEPS * PARTS * padded, LANES)
 
 
 def nn(a, b, precision=None):
@@ -191,9 +200,9 @@
 
 def fused(
     dims,
-    parent_ref, nest_ref, terrain_ref, shift_ref, bound_ref, dest_ref, inv_ref,
+    parent_ref, nest_ref, terrain_ref, shift_ref, bound_ref, dest_ref, last_ref, parts_ref,
     parent_out, nest_out, mean_out, var_out,
-    meta, halo_out, halo_in, terr_in, zg, pm, pr, w, msg, got, mine, theirs,
+    held, meta, halo_out, halo_in, terr_in, zg, pm, pr, w, msg, got, mine, theirs, held_s,
     meta_s, meta_r, halo_s, halo_r, terr_s, terr_r, z_s, z_r, p_s, p_r, msg_s, msg_r, mem_s, mem_r,
 ):
     members, levels, rows, width, cols, nb, tiles, per, cells = dims
@@ -203,6 +212,8 @@
     half = rows // 2
     me = lax.axis_index("tile")
     core = lax.axis_index("member")
+    mixed = members * levels
+    tall_mixed = held.shape[0] // rows
     my_p = lax.rem(me, PLANE)
     my_z = me // PLANE
 
@@ -220,16 +231,9 @@
         pl.semaphore_signal(barrier, inc=1, device_id=(core, at(d)), device_id_type=MESH)
     pl.semaphore_signal(barrier, inc=1, device_id=(1 - core, me), device_id_type=MESH)
 
+    fetch = pltpu.make_async_copy(parent_ref, held.at[pl.ds(0, mixed * rows)], held_s)
+    fetch.start()
     row_i = lax.broadcasted_iota(jnp.int32, (rows, width), 0)
-
-    def pack(level, _):
-        p0 = parent_ref[level]
-        p1 = parent_ref[levels + level]
-        halo_out[0, level] = jnp.where(row_i < half, pltpu.roll(p0, half, axis=0), p1)
-        halo_out[1, level] = jnp.where(row_i < half, p0, pltpu.roll(p1, half, axis=0))
-        return 0
-
-    lax.fori_loop(0, levels, pack, 0)
 
     meta[me, 0:STEPS, :] = dest_ref[...]
     meta[me, STEPS : 2 * STEPS, :] = jnp.zeros((STEPS, cols), jnp.int32)
@@ -238,9 +242,19 @@
         at_col = lax.rem(lax.rem(index, width) + shift_ref[s] + width, width)
         meta[me, STEPS + s : STEPS + s + 1, 0:nb] = (index // width) * width + at_col
 
-    last = inv_ref[STEPS - 1][:padded, :levels]
     for m in range(members):
-        zg[my_z, m] = nn(last, nest_ref[m], HI)
+        zg[my_z, m] = nn(last_ref[...], nest_ref[m], HI)
+
+    fetch.wait()
+    held[mixed * rows :, :] = jnp.zeros((held.shape[0] - mixed * rows, width), F32)
+    for i in range(2):
+        for d in range(half):
+            row = rows - 1 - d if i == 0 else d
+            field = held[pl.ds(row, tall_mixed, stride=rows), :]
+            near = field.astype(BF16)
+            halo_out[i, d * tall_mixed : (d + 1) * tall_mixed, :] = near
+            if d == 0:
+                halo_out[i, half * tall_mixed :, :] = (field - near.astype(F32)).astype(BF16)
 
     pl.semaphore_wait(barrier, tiles)
 
@@ -323,54 +337,51 @@
         path = hop if path is None else nn(path, hop).astype(BF16)
         moves[s] = path
 
-    for d in range(1, zs):
-        rcopy(
-            zg.at[my_z], zg.at[lax.rem(my_z + zs - d, zs)], z_s.at[d], z_r.at[d], me
-        ).wait_recv()
-
-    def masked(origin, m):
-        out = jnp.zeros((padded, cols), F32)
-        for z in range(zs):
-            out = jnp.where(origin == z * PLANE + my_p, zg[z, m], out)
-        return out
-
-    for d in range(1, PLANE):
-        final = my_z * PLANE + lax.rem(my_p + d, PLANE)
-        origin = chase(final)[0][0]
+    def fill(level, _):
+        own = pltpu.roll(held[pl.ds(pl.multiple_of(level * rows, rows), rows), :], half, axis=0)
+        top = jnp.where(row_i < half, 0.0, own)
+        bottom = jnp.where(row_i < half, own, 0.0)
+        w[pl.ds(pl.multiple_of(level * tall, tall), tall), :] = jnp.concatenate([top, bottom], axis=0)
+        return 0
+
+    lax.fori_loop(0, tall_mixed, fill, 0, unroll=8)
+
+    slot_rows = STEPS * CAPB
+
+    def pick(s):
+        fields = []
         for m in range(members):
-            pm[d - 1, m] = masked(origin, m)
-        start(rcopy(pm.at[d - 1], pr.at[d - 1], p_s.at[d], p_r.at[d], final))
-
+            pieces = [
+                w[pl.ds(m * levels * tall + half + r, padded, stride=tall), :] for r in range(rows)
+            ]
+            fields.append(jnp.concatenate(pieces, axis=1))
+            fields.append(jnp.zeros((LANES - padded, cells), F32))
+        values = nt(requests[s], jnp.concatenate(fields, axis=0).astype(BF16))
+        for k in range(CAPB):
+            for m in range(members):
+                msg[m, pl.ds(s * CAPB + k, tiles, stride=slot_rows), :] = values[
+                    k * tiles : (k + 1) * tiles, m * LANES : (m + 1) * LANES
+                ]
+
+    pick(0)
+
+    row_t = lax.broadcasted_iota(jnp.int32, (tall, width), 0) + me * rows - half
+    inside = jnp.logical_and(row_t >= 0, row_t < tiles * rows)
     for i in range(2):
         @pl.when(has[1 - i])
         def _():
             for copy in halo_pair(i, me):
                 copy.wait_recv()
+            for d in range(half):
+                row = half - 1 - d if i == 0 else half + rows + d
+                came = halo_in[i, d * tall_mixed : (d + 1) * tall_mixed, :].astype(F32)
+                if d == 0:
+                    came = came + halo_in[i, half * tall_mixed :, :].astype(F32)
+                w[pl.ds(row, tall_mixed, stride=tall), :] = came
 
         @pl.when(jnp.logical_not(has[1 - i]))
         def _():
-            halo_in[i] = jnp.zeros((levels, rows, width), F32)
             terr_in[i] = jnp.zeros((rows, width), jnp.int32)
-
-    row_t = lax.broadcasted_iota(jnp.int32, (tall, width), 0) + me * rows - half
-    inside = jnp.logical_and(row_t >= 0, row_t < tiles * rows)
-
-    def fill(level, _):
-        low = halo_in[0, level]
-        high = halo_in[1, level]
-        for m in range(members):
-            base = pl.multiple_of((m * levels + level) * tall, tall)
-            own = pltpu.roll(parent_ref[m * levels + level], half, axis=0)
-            lo = low if m == 0 else pltpu.roll(low, half, axis=0)
-            hi = pltpu.roll(high, half, axis=0) if m == 0 else high
-            top = jnp.where(row_i < half, lo, own)
-            bottom = jnp.where(row_i < half, own, hi)
-            w[pl.ds(base, tall), :] = jnp.concatenate([top, bottom], axis=0)
-        return 0
-
-    lax.fori_loop(0, levels, fill, 0)
-    tail = members * levels * tall
-    w[tail:, :] = jnp.zeros((w.shape[0] - tail, width), F32)
 
     terr = terrain_ref[...]
     terr_own = pltpu.roll(terr, half, axis=0)
@@ -404,7 +415,7 @@
                     )
                     new = centre * cur + HORIZ_MIX * sides + VERT_MIX * (up + before[m])
                     if final:
-                        parent_out[m * levels + level] = new[half : half + rows]
+                        parent_out[pl.ds(pl.multiple_of((m * levels + level) * rows, rows), rows), :] = new[half : half + rows]
                     else:
                         w[pl.ds(base, tall), :] = jnp.where(inside, new, 0.0)
                     before[m] = cur
@@ -413,31 +424,37 @@
         first = tuple(w[m * levels * tall : (m * levels + 1) * tall, :] for m in range(members))
         lax.fori_loop(0, levels // chunk, body, first)
 
-    slot_rows = members * STEPS * CAPB
-
-    def pick(s):
+    advance(False)
+    pick(1)
+
+    for d in range(1, zs):
+        rcopy(
+            zg.at[my_z], zg.at[lax.rem(my_z + zs - d, zs)], z_s.at[d], z_r.at[d], me
+        ).wait_recv()
+
+    def masked(origin, m):
+        out = jnp.zeros((padded, cols), F32)
+        for z in range(zs):
+            out = jnp.where(origin == z * PLANE + my_p, zg[z, m], out)
+        return out
+
+    for d in range(1, PLANE):
+        final = my_z * PLANE + lax.rem(my_p + d, PLANE)
+        origin = chase(final)[0][0]
         for m in range(members):
-            pieces = [
-                w[pl.ds(m * levels * tall + half + r, padded, stride=tall), :] for r in range(rows)
-            ]
-            field = jnp.concatenate(pieces, axis=1)
-            field = jnp.concatenate([field, jnp.zeros((LANES - padded, cells), F32)], axis=0)
-            values = nt(requests[s], field.astype(BF16))
-            for k in range(CAPB):
-                slot = m * STEPS * CAPB + s * CAPB + k
-                msg[pl.ds(slot, tiles, stride=slot_rows), :] = values[k * tiles : (k + 1) * tiles]
-
-    for s in range(STEPS - 1):
+            pm[d - 1, m] = masked(origin, m)
+        start(rcopy(pm.at[d - 1], pr.at[d - 1], p_s.at[d], p_r.at[d], final))
+
+    for s in range(2, STEPS):
+        advance(False)
         pick(s)
-        advance(False)
-    pick(STEPS - 1)
 
     def rows_of(tile):
         return pl.ds(pl.multiple_of(tile * slot_rows, slot_rows), slot_rows)
 
     for d in range(1, tiles):
-        start(rcopy(msg.at[rows_of(at(d))], got.at[rows_of(me)], msg_s.at[d], msg_r.at[d], at(d)))
-    got[rows_of(me), :] = msg[rows_of(me), :]
+        start(rcopy(msg.at[:, rows_of(at(d))], got.at[:, rows_of(me)], msg_s.at[d], msg_r.at[d], at(d)))
+    got[:, rows_of(me), :] = msg[:, rows_of(me), :]
 
     advance(True)
 
@@ -453,34 +470,55 @@
         result.append(nt(block, moves[0].astype(F32), HI))
 
     g_rows = tiles * slot_rows
-    g_iota = lax.broadcasted_iota(jnp.int32, (g_rows, cols), 0)
-    g_lane = lax.broadcasted_iota(jnp.int32, (g_rows, cols), 1)
-    g_owner = g_iota // slot_rows
-    g_slot = lax.rem(g_iota, slot_rows)
-    takes = [[None] * STEPS for _ in range(members)]
+    lane_1 = lax.broadcasted_iota(jnp.int32, (SUB, LANES), 1)
+    row_1 = lax.broadcasted_iota(jnp.int32, (SUB, cols), 0)
+    lane_j = lax.broadcasted_iota(jnp.int32, (SUB, cols), 1)
+    weight = jnp.zeros((SUB, LANES), F32)
+    place = jnp.zeros((SUB, LANES), F32)
     for s in range(STEPS):
         asker = sources[s][:, 0:1]
         cell = jnp.sum(
             jnp.where(t_iota == asker, meta[:, STEPS + s, :], 0), axis=0, keepdims=True
         )
-        ours = jnp.logical_and(g_owner == cell // cells, g_lane < nb)
-        for m in range(members):
-            slot = m * STEPS * CAPB + s * CAPB + lax.rem(g_lane, CAPB)
-            takes[m][s] = nt(
-                one_hot(jnp.logical_and(ours, g_slot == slot)), moves[s]
-            ).astype(BF16)
+        fed = (cell // cells) * slot_rows + s * CAPB + lax.rem(lane_j, CAPB)
+        table = jnp.where(row_1 == 0, 1, fed)
+        table = jnp.where(lane_j < nb, table, 0).astype(F32).astype(BF16)
+        hot = jnp.where(moves[s] > 0, 1.0, 0.0).astype(BF16)
+        here = lane_1 // per == s
+        moved = pltpu.roll(nt(table, moves[s])[:, :LANES], s * per, axis=1)
+        weight = jnp.where(here, moved, weight)
+        moved = pltpu.roll(nt(table, hot)[:, :LANES], s * per, axis=1)
+        place = jnp.where(here, moved, place)
+    place = place[1:2].astype(jnp.int32)
+    g_iota = lax.broadcasted_iota(jnp.int32, (g_rows, LANES), 0)
+    takes = jnp.where(g_iota == place, weight[0:1], 0.0).astype(BF16)
 
     for d in range(1, tiles):
         rcopy(
-            msg.at[rows_of(me)], got.at[rows_of(at(tiles - d))], msg_s.at[d], msg_r.at[d], me
+            msg.at[:, rows_of(me)], got.at[:, rows_of(at(tiles - d))], msg_s.at[d], msg_r.at[d], me
         ).wait_recv()
-    arrived = jnp.transpose(got[...]).astype(BF16)
+    entries = [nn(jnp.transpose(got[m]).astype(BF16), takes).astype(BF16) for m in range(members)]
+    solved = nn(parts_ref[...], jnp.concatenate(entries, axis=1))
+    lane_p = lax.broadcasted_iota(jnp.int32, (padded, LANES), 1)
     for m in range(members):
+        added = jnp.zeros((padded, LANES), F32)
         for s in range(STEPS):
-            entry = nn(arrived, takes[m][s])
-            result[m] = result[m] + nn(inv_ref[STEPS - 1 - s], entry, HI)[:padded]
-        mine[m] = result[m]
-        nest_out[m] = result[m][:levels]
+            terms = [
+                solved[(s * PARTS + part) * padded : (s * PARTS + part + 1) * padded,
+                       m * LANES : (m + 1) * LANES]
+                for part in range(PARTS)
+            ]
+            added = jnp.where(lane_p // per == s, terms[0] + (terms[1] + terms[2]), added)
+        span = LANES // 2
+        while span >= per:
+            added = added + pltpu.roll(added, span, axis=1)
+            span //= 2
+        added = jnp.where(lane_p < per, added, 0.0)
+        if cols > LANES:
+            added = jnp.concatenate([added, jnp.zeros((padded, cols - LANES), F32)], axis=1)
+        full = result[m] + added
+        mine[m] = full
+        nest_out[m] = full[:levels]
 
     pair = rcopy(mine, theirs, mem_s, mem_r, me, 1 - core)
     pair.start()
@@ -509,33 +547,38 @@
     cells = rows * width
     padded = -(-levels // 8) * 8
     zs = tiles // PLANE
-    slot_rows = members * STEPS * CAPB
+    slot_rows = STEPS * CAPB
+    mixed = members * levels
+    tall_mixed = -(-mixed // SUB) * SUB
     dims = (members, levels, rows, width, cols, nb, tiles, cols // (tiles // 2), cells)
     vmem = pl.BlockSpec(memory_space=pltpu.VMEM)
     dma = pltpu.SemaphoreType.DMA
+    last, parts = inverse_powers(levels)
     outs = pl.pallas_call(
         functools.partial(fused, dims),
         out_shape=(
-            jax.ShapeDtypeStruct((members * levels, rows, width), F32),
+            jax.ShapeDtypeStruct((mixed * rows, width), F32),
             jax.ShapeDtypeStruct((members, levels, cols), F32),
             jax.ShapeDtypeStruct((levels, cols), F32),
             jax.ShapeDtypeStruct((levels, cols), F32),
         ),
-        in_specs=[vmem, vmem, vmem, pl.BlockSpec(memory_space=pltpu.SMEM), vmem, vmem, vmem],
+        in_specs=[pl.BlockSpec(memory_space=pltpu.HBM), vmem, vmem, pl.BlockSpec(memory_space=pltpu.SMEM)] + [vmem] * 4,
         out_specs=(vmem,) * 4,
         scratch_shapes=[
+            pltpu.VMEM((tall_mixed * rows, width), F32),
             pltpu.VMEM((tiles, 2 * STEPS, cols), jnp.int32),
-            pltpu.VMEM((2, levels, rows, width), F32),
-            pltpu.VMEM((2, levels, rows, width), F32),
+            pltpu.VMEM((2, (rows // 2 + 1) * tall_mixed, width), BF16),
+            pltpu.VMEM((2, (rows // 2 + 1) * tall_mixed, width), BF16),
             pltpu.VMEM((2, rows, width), jnp.int32),
             pltpu.VMEM((zs, members, padded, cols), F32),
             pltpu.VMEM((PLANE - 1, members, padded, cols), F32),
             pltpu.VMEM((PLANE - 1, members, padded, cols), F32),
-            pltpu.VMEM(((members * levels + padded - levels) * 2 * rows, width), F32),
-            pltpu.VMEM((tiles * slot_rows, LANES), F32),
-            pltpu.VMEM((tiles * slot_rows, LANES), F32),
+            pltpu.VMEM((tall_mixed * 2 * rows, width), F32),
+            pltpu.VMEM((members, tiles * slot_rows, LANES), F32),
+            pltpu.VMEM((members, tiles * slot_rows, LANES), F32),
             pltpu.VMEM((members, padded, cols), F32),
             pltpu.VMEM((members, padded, cols), F32),
+            dma,
             dma((tiles,)), dma((tiles,)),
             dma((2,)), dma((2,)), dma((2,)), dma((2,)),
             dma((zs,)), dma((zs,)), dma((PLANE,)), dma((PLANE,)),
@@ -543,12 +586,12 @@
             dma, dma,
         ],
         compiler_params=pltpu.CompilerParams(
-            collective_id=0, has_side_effects=True, vmem_limit_bytes=48 * 1024 * 1024
+            collective_id=0, has_side_effects=True, vmem_limit_bytes=63 * 1024 * 1024
         ),
     )(
-        parent_state.reshape(members * levels, rows, width),
+        parent_state.reshape(mixed * rows, width),
         nest_state, terrain, shift_x, boundary_index, reloc_dest,
-        jnp.asarray(inverse_powers(levels)),
+        jnp.asarray(last), jnp.asarray(parts),
     )
     return (outs[0].reshape(parent_state.shape),) + tuple(outs[1:])
 
@@ -565,6 +608,7 @@
         and parent[2] // tiles == 2 * STEPS
         and parent[3] == LANES
         and cols % LANES == 0
+        and STEPS * (cols // (tiles // 2)) == LANES
     )
 
 

time: 56.8 us -> 54.4 us (0.958)
  Pallas kernels: 50.9 us -> 46.6 us
  local copies, waits for them, and re-layouts: 4.94 us -> 6.84 us
    pallas_call x1, Pallas kernels: 50.9 us -> 46.6 us  [on_device_fused(): pl.pallas_call(functools.partial(fused, dims), out_shape=(jax.ShapeDtypeS...]
    unnamed x17 -> x9, local copies, waits for them, and re-layouts: 4.94 us -> 6.84 us
where the time goes in v2:
time: 54.4 us; the launch traced here: 54.1 us
  Pallas kernels  46.6 us (86%)
  local copies, waits for them, and re-layouts  6.84 us (13%)
  between operations  0.64 us (1%)
    pallas_call x1, Pallas kernels, on_device_fused(): pl.pallas_call(functools.partial(fused, dims), out_shape=(jax.ShapeDtypeS...  46.6 us
    unnamed x9, local copies, waits for them, and re-layouts  6.84 us

profile of v2, /device:TPU:0, one launch (start us, length us, event | category | flops | bytes accessed | tf_op | source)
XLA Modules:
  0.0 54.1 jit_solution(3338733432134023095)
XLA Ops:
  0.6 1.6 %copy.12.nest_ref = f32[2,81,256]{2,1,0:T(8,128)} copy(f32[2,81,256]{2,0,1:T(2,128)} %param.9) | data formatting | bytes 331776 | tf_op args[1]
  2.2 46.6 %shard_map.111 = (f32[1296,128]{1,0:T(8,128)}, f32[2,81,256]{2,1,0:T(8,128)}, f32[81,256]{1,0:T(8,128)}, f32[81,256]{1,0:T(8,128)}) custom-call(f32[1296,128]{1,0:T(8,128)} %bitcast.2, f32[2,81,256]{2,1,0:T(8,128)} %copy.12.nest_ref, s32[8,128]{1,0:T(8,128)} %terrain_ref.1, s32[4]{0:T(128)} %shift_ref.1, s32[4,16]{1,0:T(4,128)} %bound_ref.1, ...), custom_call_target="tpu_custom_call" | custom-call | tf_op jit(solution)/shard_map/pallas_call | solution.py:557
  48.8 1.7 %copy.13 = f32[2,81,256]{2,0,1:T(2,128)} copy(f32[2,81,256]{2,1,0:T(8,128)} %get-tuple-element.13) | data formatting | bytes 331776
  50.5 0.0 copy-start.1
  50.5 2.0 %copy.17 = f32[2,81,8,128]{3,2,1,0:T(8,128)} copy(f32[2,81,8,128]{3,2,1,0:T(8,128)} %bitcast.3) | data formatting | bytes 1327104
  52.5 0.0 copy-done.1
  52.5 0.0 copy-start
  52.5 0.6 %copy.18 = f32[81,256]{1,0:T(8,128)} copy(f32[81,256]{1,0:T(8,128)S(1)} %copy-done.1) | data formatting | bytes 165888
  53.2 0.3 copy-done
  53.5 0.6 %copy.19 = f32[81,256]{1,0:T(8,128)} copy(f32[81,256]{1,0:T(8,128)S(1)} %copy-done) | data formatting | bytes 165888
Async XLA Ops:
  50.5 2.0 %copy-start.1 = (f32[81,256]{1,0:T(8,128)S(1)}, f32[81,256]{1,0:T(8,128)}, u32[]{:S(2)}) copy-start(f32[81,256]{1,0:T(8,128)} %get-tuple-element.22) | copy-start | bytes 248836
  52.5 0.9 %copy-start = (f32[81,256]{1,0:T(8,128)S(1)}, f32[81,256]{1,0:T(8,128)}, u32[]{:S(2)}) copy-start(f32[81,256]{1,0:T(8,128)} %get-tuple-element.23) | copy-start | bytes 248836

commit v3 on v2

--- a/solution.py
+++ b/solution.py
@@ -156,6 +156,7 @@
 LANES = 128
 PARTS = 3
 SUB = 16
+EDGE = 8
 
 
 def inverse_powers(levels):
@@ -202,7 +203,7 @@
     dims,
     parent_ref, nest_ref, terrain_ref, shift_ref, bound_ref, dest_ref, last_ref, parts_ref,
     parent_out, nest_out, mean_out, var_out,
-    held, meta, halo_out, halo_in, terr_in, zg, pm, pr, w, msg, got, mine, theirs, held_s,
+    meta, halo_out, halo_in, terr_in, zg, pm, pr, w, msg, got, mine, theirs,
     meta_s, meta_r, halo_s, halo_r, terr_s, terr_r, z_s, z_r, p_s, p_r, msg_s, msg_r, mem_s, mem_r,
 ):
     members, levels, rows, width, cols, nb, tiles, per, cells = dims
@@ -212,8 +213,7 @@
     half = rows // 2
     me = lax.axis_index("tile")
     core = lax.axis_index("member")
-    mixed = members * levels
-    tall_mixed = held.shape[0] // rows
+    both = members * padded
     my_p = lax.rem(me, PLANE)
     my_z = me // PLANE
 
@@ -230,10 +230,6 @@
     for d in range(1, tiles):
         pl.semaphore_signal(barrier, inc=1, device_id=(core, at(d)), device_id_type=MESH)
     pl.semaphore_signal(barrier, inc=1, device_id=(1 - core, me), device_id_type=MESH)
-
-    fetch = pltpu.make_async_copy(parent_ref, held.at[pl.ds(0, mixed * rows)], held_s)
-    fetch.start()
-    row_i = lax.broadcasted_iota(jnp.int32, (rows, width), 0)
 
     meta[me, 0:STEPS, :] = dest_ref[...]
     meta[me, STEPS : 2 * STEPS, :] = jnp.zeros((STEPS, cols), jnp.int32)
@@ -243,18 +239,28 @@
         meta[me, STEPS + s : STEPS + s + 1, 0:nb] = (index // width) * width + at_col
 
     for m in range(members):
-        zg[my_z, m] = nn(last_ref[...], nest_ref[m], HI)
-
-    fetch.wait()
-    held[mixed * rows :, :] = jnp.zeros((held.shape[0] - mixed * rows, width), F32)
+        zg[my_z, m] = nn(last_ref[...], nest_ref[:, m, :], HI)
+
+    tail = jnp.zeros((w.shape[3] - EDGE - padded + EDGE, width), F32)
+    for t in range(STEPS):
+        for r in range(tall):
+            for m in range(members):
+                w[t, r, m, padded:, :] = tail
+    for r in range(rows):
+        for m in range(members):
+            w[0, half + r, m, EDGE : EDGE + levels, :] = parent_ref[
+                pl.ds(m * levels * rows + r, levels, stride=rows), :
+            ]
     for i in range(2):
         for d in range(half):
-            row = rows - 1 - d if i == 0 else d
-            field = held[pl.ds(row, tall_mixed, stride=rows), :]
+            row = half + (rows - 1 - d if i == 0 else d)
+            field = jnp.concatenate(
+                [w[0, row, m, EDGE : EDGE + padded, :] for m in range(members)], axis=0
+            )
             near = field.astype(BF16)
-            halo_out[i, d * tall_mixed : (d + 1) * tall_mixed, :] = near
+            halo_out[i, d * both : (d + 1) * both, :] = near
             if d == 0:
-                halo_out[i, half * tall_mixed :, :] = (field - near.astype(F32)).astype(BF16)
+                halo_out[i, half * both :, :] = (field - near.astype(F32)).astype(BF16)
 
     pl.semaphore_wait(barrier, tiles)
 
@@ -303,27 +309,27 @@
 
     lane_t = lax.broadcasted_iota(jnp.int32, (tiles, LANES), 1)
     lane_c = lax.broadcasted_iota(jnp.int32, (tiles, cols), 1)
-    cell_iota = lax.broadcasted_iota(jnp.int32, (tiles, cells), 1)
-    eye = one_hot(lax.broadcasted_iota(jnp.int32, (LANES, LANES), 0)
-                  == lax.broadcasted_iota(jnp.int32, (LANES, LANES), 1))
-    requests = [None] * STEPS
+    slot_rows = STEPS * CAPB
+    wanted = jnp.zeros((1, LANES), jnp.int32)
     path = None
     for s in range(STEPS - 1, -1, -1):
-        hop = one_hot(dest_tile[s][:, 0:1] == lane_t)
-        hop = jnp.concatenate([hop, jnp.zeros((LANES - tiles, LANES), BF16)], axis=0)
-        path = hop if path is None else nn(hop, path).astype(BF16)
-        back = nt(eye, path).astype(BF16)[0:tiles, :]
+        hop = one_hot(dest_tile[s][:, 0:1] == lane_t // slot_rows)
+        if path is None:
+            path = hop
+        else:
+            step_hop = one_hot(dest_tile[s][:, 0:1] == lane_t)
+            above = jnp.concatenate([path, jnp.zeros((LANES - tiles, LANES), BF16)], axis=0)
+            path = nn(step_hop, above).astype(BF16)
         cell = meta[:, STEPS + s, :]
         owned = jnp.logical_and(cell // cells == me, lane_c < nb)
         local = lax.rem(cell, cells) + 1
-        parts = []
         for k in range(CAPB):
-            pick = jnp.logical_and(owned, lax.rem(lane_c, CAPB) == k)
-            which = jnp.sum(jnp.where(pick, local, 0), axis=1, keepdims=True) - 1
-            asked = one_hot(cell_iota == which)
-            asked = jnp.concatenate([asked, jnp.zeros((LANES - tiles, cells), BF16)], axis=0)
-            parts.append(nn(back, asked).astype(BF16))
-        requests[s] = jnp.concatenate(parts, axis=0)
+            pick_k = jnp.logical_and(owned, lax.rem(lane_c, CAPB) == k)
+            which = jnp.sum(jnp.where(pick_k, local, 0), axis=1, keepdims=True)
+            there = jnp.logical_and(path > 0, lax.rem(lane_t, slot_rows) == s * CAPB + k)
+            wanted = wanted + jnp.sum(jnp.where(there, which, 0), axis=0, keepdims=True)
+    cell_iota = lax.broadcasted_iota(jnp.int32, (cells, LANES), 0)
+    requests = one_hot(cell_iota == wanted - 1)
 
     sources, slots = chase(me)
 
@@ -337,36 +343,73 @@
         path = hop if path is None else nn(path, hop).astype(BF16)
         moves[s] = path
 
-    def fill(level, _):
-        own = pltpu.roll(held[pl.ds(pl.multiple_of(level * rows, rows), rows), :], half, axis=0)
-        top = jnp.where(row_i < half, 0.0, own)
-        bottom = jnp.where(row_i < half, own, 0.0)
-        w[pl.ds(pl.multiple_of(level * tall, tall), tall), :] = jnp.concatenate([top, bottom], axis=0)
-        return 0
-
-    lax.fori_loop(0, tall_mixed, fill, 0, unroll=8)
-
-    slot_rows = STEPS * CAPB
-
-    def pick(s):
-        fields = []
+    lane_s = lax.rem(lax.broadcasted_iota(jnp.int32, (both, LANES), 1), slot_rows) // CAPB
+    picked = [jnp.zeros((both, LANES), F32)]
+
+    def pick(t):
+        field = jnp.concatenate(
+            [
+                jnp.concatenate(
+                    [w[t, half + r, m, EDGE : EDGE + padded, :] for m in range(members)], axis=0
+                ).astype(BF16)
+                for r in range(rows)
+            ],
+            axis=1,
+        )
+        picked[0] = jnp.where(lane_s == t, nn(field, requests), picked[0])
+
+    pick(0)
+
+    def coefficient(terr_row):
+        return 1.0 - 4.0 * HORIZ_MIX - 2.0 * VERT_MIX - DRAG_RATE * terr_row.astype(F32) / 3000.0
+
+    def centre_of(r):
+        if r < half:
+            return coefficient(terr_in[0, rows - half + r : rows - half + r + 1, :])
+        if r < half + rows:
+            return coefficient(terrain_ref[r - half : r - half + 1, :])
+        return coefficient(terr_in[1, r - half - rows : r - half - rows + 1, :])
+
+    def guard(t, r):
         for m in range(members):
-            pieces = [
-                w[pl.ds(m * levels * tall + half + r, padded, stride=tall), :] for r in range(rows)
+            w[t, r, m, EDGE - 1 : EDGE, :] = w[t, r, m, EDGE : EDGE + 1, :]
+            w[t, r, m, EDGE + levels : EDGE + levels + 1, :] = w[
+                t, r, m, EDGE + levels - 1 : EDGE + levels, :
             ]
-            fields.append(jnp.concatenate(pieces, axis=1))
-            fields.append(jnp.zeros((LANES - padded, cells), F32))
-        values = nt(requests[s], jnp.concatenate(fields, axis=0).astype(BF16))
-        for k in range(CAPB):
-            for m in range(members):
-                msg[m, pl.ds(s * CAPB + k, tiles, stride=slot_rows), :] = values[
-                    k * tiles : (k + 1) * tiles, m * LANES : (m + 1) * LANES
-                ]
-
-    pick(0)
-
-    row_t = lax.broadcasted_iota(jnp.int32, (tall, width), 0) + me * rows - half
-    inside = jnp.logical_and(row_t >= 0, row_t < tiles * rows)
+
+    def advance(t, r):
+        centre = centre_of(r)
+        beyond = None
+        if r < half:
+            beyond = jnp.where(has[1], 1.0, 0.0)
+        elif r >= half + rows:
+            beyond = jnp.where(has[0], 1.0, 0.0)
+        guard(t, r)
+        for m in range(members):
+            cur = w[t, r, m, EDGE : EDGE + padded, :]
+            up = w[t, r, m, EDGE + 1 : EDGE + 1 + padded, :]
+            down = w[t, r, m, EDGE - 1 : EDGE - 1 + padded, :]
+            north = w[t, r + 1, m, EDGE : EDGE + padded, :]
+            south = w[t, r - 1, m, EDGE : EDGE + padded, :]
+            sides = (north + south) + (pltpu.roll(cur, 1, axis=1) + pltpu.roll(cur, width - 1, axis=1))
+            new = centre * cur + HORIZ_MIX * sides + VERT_MIX * (up + down)
+            if beyond is not None:
+                new = new * beyond
+            if t == STEPS - 1:
+                parent_out[pl.ds(m * levels * rows + r - half, levels, stride=rows), :] = new[:levels]
+            else:
+                w[t + 1, r, m, EDGE : EDGE + padded, :] = new
+
+    for t in range(STEPS - 1):
+        for r in range(half + t + 1, half + rows - t - 1):
+            advance(t, r)
+
+    def outer(t):
+        inner = range(half + t + 1, half + rows - t - 1)
+        for r in range(t + 1, tall - t - 1):
+            if r not in inner:
+                advance(t, r)
+
     for i in range(2):
         @pl.when(has[1 - i])
         def _():
@@ -374,57 +417,21 @@
                 copy.wait_recv()
             for d in range(half):
                 row = half - 1 - d if i == 0 else half + rows + d
-                came = halo_in[i, d * tall_mixed : (d + 1) * tall_mixed, :].astype(F32)
+                came = halo_in[i, d * both : (d + 1) * both, :].astype(F32)
                 if d == 0:
-                    came = came + halo_in[i, half * tall_mixed :, :].astype(F32)
-                w[pl.ds(row, tall_mixed, stride=tall), :] = came
+                    came = came + halo_in[i, half * both :, :].astype(F32)
+                for m in range(members):
+                    w[0, row, m, EDGE : EDGE + padded, :] = came[m * padded : (m + 1) * padded]
 
         @pl.when(jnp.logical_not(has[1 - i]))
         def _():
             terr_in[i] = jnp.zeros((rows, width), jnp.int32)
-
-    terr = terrain_ref[...]
-    terr_own = pltpu.roll(terr, half, axis=0)
-    terr_all = jnp.concatenate(
-        [
-            jnp.where(row_i < half, pltpu.roll(terr_in[0], half, axis=0), terr_own),
-            jnp.where(row_i < half, terr_own, pltpu.roll(terr_in[1], half, axis=0)),
-        ],
-        axis=0,
-    )
-    damping = DRAG_RATE * terr_all.astype(F32) / 3000.0
-    centre = 1.0 - 4.0 * HORIZ_MIX - 2.0 * VERT_MIX - damping
-
-    chunk = 9 if levels % 9 == 0 else 1
-
-    def advance(final):
-        def body(c, before):
-            before = list(before)
-            for u in range(chunk):
-                level = c * chunk + u
+            for d in range(half):
+                row = half - 1 - d if i == 0 else half + rows + d
                 for m in range(members):
-                    base = pl.multiple_of((m * levels + level) * tall, tall)
-                    above = pl.multiple_of(
-                        (m * levels + jnp.minimum(level + 1, levels - 1)) * tall, tall
-                    )
-                    cur = w[pl.ds(base, tall), :]
-                    up = w[pl.ds(above, tall), :]
-                    sides = (
-                        pltpu.roll(cur, 1, axis=0) + pltpu.roll(cur, tall - 1, axis=0)
-                        + pltpu.roll(cur, 1, axis=1) + pltpu.roll(cur, width - 1, axis=1)
-                    )
-                    new = centre * cur + HORIZ_MIX * sides + VERT_MIX * (up + before[m])
-                    if final:
-                        parent_out[pl.ds(pl.multiple_of((m * levels + level) * rows, rows), rows), :] = new[half : half + rows]
-                    else:
-                        w[pl.ds(base, tall), :] = jnp.where(inside, new, 0.0)
-                    before[m] = cur
-            return tuple(before)
-
-        first = tuple(w[m * levels * tall : (m * levels + 1) * tall, :] for m in range(members))
-        lax.fori_loop(0, levels // chunk, body, first)
-
-    advance(False)
+                    w[0, row, m, EDGE : EDGE + padded, :] = jnp.zeros((padded, width), F32)
+
+    outer(0)
     pick(1)
 
     for d in range(1, zs):
@@ -445,9 +452,13 @@
             pm[d - 1, m] = masked(origin, m)
         start(rcopy(pm.at[d - 1], pr.at[d - 1], p_s.at[d], p_r.at[d], final))
 
-    for s in range(2, STEPS):
-        advance(False)
-        pick(s)
+    for t in range(2, STEPS):
+        outer(t - 1)
+        pick(t)
+    for m in range(members):
+        part = picked[0][m * padded : (m + 1) * padded]
+        part = jnp.concatenate([part, jnp.zeros((LANES - padded, LANES), F32)], axis=0)
+        msg[m] = jnp.transpose(part)
 
     def rows_of(tile):
         return pl.ds(pl.multiple_of(tile * slot_rows, slot_rows), slot_rows)
@@ -456,7 +467,8 @@
         start(rcopy(msg.at[:, rows_of(at(d))], got.at[:, rows_of(me)], msg_s.at[d], msg_r.at[d], at(d)))
     got[:, rows_of(me), :] = msg[:, rows_of(me), :]
 
-    advance(True)
+    for r in range(half, half + rows):
+        advance(STEPS - 1, r)
 
     origin = sources[0]
     for d in range(1, PLANE):
@@ -539,6 +551,20 @@
                 copy.wait_send()
 
 
+def write_out(parent_ref, nest_ref, mean_ref, var_ref, parent_out, nest_out, mean_out, var_out, sems):
+    copies = [
+        pltpu.make_async_copy(parent_ref, parent_out, sems.at[0]),
+        pltpu.make_async_copy(mean_ref, mean_out, sems.at[1]),
+        pltpu.make_async_copy(var_ref, var_out, sems.at[2]),
+    ]
+    for copy in copies:
+        copy.start()
+    for m in range(nest_ref.shape[0]):
+        nest_out[:, m, :] = nest_ref[m]
+    for copy in copies:
+        copy.wait()
+
+
 def on_device_fused(parent_state, nest_state, terrain, shift_x, boundary_index, reloc_dest):
     members, levels, rows, width = parent_state.shape
     cols = nest_state.shape[2]
@@ -549,7 +575,7 @@
     zs = tiles // PLANE
     slot_rows = STEPS * CAPB
     mixed = members * levels
-    tall_mixed = -(-mixed // SUB) * SUB
+    both = members * padded
     dims = (members, levels, rows, width, cols, nb, tiles, cols // (tiles // 2), cells)
     vmem = pl.BlockSpec(memory_space=pltpu.VMEM)
     dma = pltpu.SemaphoreType.DMA
@@ -562,23 +588,21 @@
             jax.ShapeDtypeStruct((levels, cols), F32),
             jax.ShapeDtypeStruct((levels, cols), F32),
         ),
-        in_specs=[pl.BlockSpec(memory_space=pltpu.HBM), vmem, vmem, pl.BlockSpec(memory_space=pltpu.SMEM)] + [vmem] * 4,
+        in_specs=[vmem, vmem, vmem, pl.BlockSpec(memory_space=pltpu.SMEM)] + [vmem] * 4,
         out_specs=(vmem,) * 4,
         scratch_shapes=[
-            pltpu.VMEM((tall_mixed * rows, width), F32),
             pltpu.VMEM((tiles, 2 * STEPS, cols), jnp.int32),
-            pltpu.VMEM((2, (rows // 2 + 1) * tall_mixed, width), BF16),
-            pltpu.VMEM((2, (rows // 2 + 1) * tall_mixed, width), BF16),
+            pltpu.VMEM((2, (rows // 2 + 1) * both, width), BF16),
+            pltpu.VMEM((2, (rows // 2 + 1) * both, width), BF16),
             pltpu.VMEM((2, rows, width), jnp.int32),
             pltpu.VMEM((zs, members, padded, cols), F32),
             pltpu.VMEM((PLANE - 1, members, padded, cols), F32),
             pltpu.VMEM((PLANE - 1, members, padded, cols), F32),
-            pltpu.VMEM((tall_mixed * 2 * rows, width), F32),
+            pltpu.VMEM((STEPS, 2 * rows, members, padded + 2 * EDGE, width), F32),
             pltpu.VMEM((members, tiles * slot_rows, LANES), F32),
             pltpu.VMEM((members, tiles * slot_rows, LANES), F32),
             pltpu.VMEM((members, padded, cols), F32),
             pltpu.VMEM((members, padded, cols), F32),
-            dma,
             dma((tiles,)), dma((tiles,)),
             dma((2,)), dma((2,)), dma((2,)), dma((2,)),
             dma((zs,)), dma((zs,)), dma((PLANE,)), dma((PLANE,)),
@@ -586,14 +610,29 @@
             dma, dma,
         ],
         compiler_params=pltpu.CompilerParams(
-            collective_id=0, has_side_effects=True, vmem_limit_bytes=63 * 1024 * 1024
+            collective_id=0, has_side_effects=True, vmem_limit_bytes=32 * 1024 * 1024
         ),
     )(
         parent_state.reshape(mixed * rows, width),
-        nest_state, terrain, shift_x, boundary_index, reloc_dest,
+        jnp.transpose(nest_state, (1, 0, 2)), terrain, shift_x, boundary_index, reloc_dest,
         jnp.asarray(last), jnp.asarray(parts),
     )
-    return (outs[0].reshape(parent_state.shape),) + tuple(outs[1:])
+    hbm = pl.BlockSpec(memory_space=pl.ANY)
+    outs = pl.pallas_call(
+        write_out,
+        out_shape=(
+            jax.ShapeDtypeStruct((mixed * rows, width), F32),
+            jax.ShapeDtypeStruct((levels, members, cols), F32),
+            jax.ShapeDtypeStruct((levels, cols), F32),
+            jax.ShapeDtypeStruct((levels, cols), F32),
+        ),
+        in_specs=[vmem] * 4,
+        out_specs=(hbm, vmem, hbm, hbm),
+        scratch_shapes=[dma((3,))],
+        compiler_params=pltpu.CompilerParams(vmem_limit_bytes=16 * 1024 * 1024),
+    )(*outs)
+    nest_field = jnp.transpose(outs[1], (1, 0, 2))
+    return (outs[0].reshape(parent_state.shape), nest_field, outs[2], outs[3])
 
 
 def fits_one_plane_split(mesh, parent, nest, bound):

time: 54.4 us -> 51.6 us (0.949)
  the two profiles are of different devices: /device:TPU:0 before, /device:TPU:15 now
where the time goes in v3:
time: 51.6 us; the launch traced here: 51.3 us
  Pallas kernels  44.8 us (87%)
  local copies, waits for them, and re-layouts  5.79 us (11%)
  between operations  0.66 us (1%)
    pallas_call x1, Pallas kernels, on_device_fused(): pl.pallas_call(functools.partial(fused, dims), out_shape=(jax.ShapeDtypeS...  43.2 us
    unnamed x16, local copies, waits for them, and re-layouts  5.79 us
    pallas_call x1, Pallas kernels, on_device_fused(): pl.pallas_call(write_out, out_shape=(jax.ShapeDtypeStruct((mixed * rows,...  1.58 us

profile of v3, /device:TPU:15, one launch (start us, length us, event | category | flops | bytes accessed | tf_op | source)
XLA Modules:
  0.0 51.3 jit_solution(4546680851376826347)
XLA Ops:
  0.6 0.0 copy-start.6
  0.6 0.0 copy-start.7
  0.7 0.7 %copy-done.6 = s32[4,16]{1,0:T(4,128)S(1)} copy-done((s32[4,16]{1,0:T(4,128)S(1)}, s32[4,16]{1,0:T(4,128)}, u32[]{:S(2)}) %copy-start.6) | copy-done | bytes 280
  1.3 0.0 copy-done.7
  1.3 0.0 copy-start
  1.3 1.1 %copy-done = f32[2,81,8,128]{3,2,1,0:T(8,128)S(1)} copy-done((f32[2,81,8,128]{3,2,1,0:T(8,128)S(1)}, f32[2,81,8,128]{3,2,1,0:T(8,128)}, u32[]{:S(2)}) %copy-start) | copy-done | bytes 663576
  2.4 0.0 copy-start.1
  2.4 1.0 %copy-done.1 = bf16[1056,128]{1,0:T(8,128)(2,1)S(1)} copy-done((bf16[1056,128]{1,0:T(8,128)(2,1)S(1)}, bf16[1056,128]{1,0:T(8,128)(2,1)}, u32[]{:S(2)}) %copy-start.1) | copy-done | bytes 270360
  3.4 0.0 copy-start.2
  3.4 0.9 %copy-done.2 = f32[2,81,256]{2,0,1:T(2,128)S(1)} copy-done((f32[2,81,256]{2,0,1:T(2,128)S(1)}, f32[2,81,256]{2,0,1:T(2,128)}, u32[]{:S(2)}) %copy-start.2) | copy-done | bytes 165912
  4.3 0.0 copy-start.3
  4.3 0.8 %copy-done.3 = f32[88,81]{1,0:T(8,128)S(1)} copy-done((f32[88,81]{1,0:T(8,128)S(1)}, f32[88,81]{1,0:T(8,128)}, u32[]{:S(2)}) %copy-start.3) | copy-done | bytes 28536
  5.1 0.0 copy-start.4
  5.1 0.7 %copy-done.4 = s32[8,128]{1,0:T(8,128)S(1)} copy-done((s32[8,128]{1,0:T(8,128)S(1)}, s32[8,128]{1,0:T(8,128)}, u32[]{:S(2)}) %copy-start.4) | copy-done | bytes 4120
  5.8 0.0 copy-start.5
  5.8 0.7 %copy-done.5 = s32[4,256]{1,0:T(4,128)S(1)} copy-done((s32[4,256]{1,0:T(4,128)S(1)}, s32[4,256]{1,0:T(4,128)}, u32[]{:S(2)}) %copy-start.5) | copy-done | bytes 4120
  6.4 43.2 %shard_map.111 = (f32[1296,128]{1,0:T(8,128)S(1)}, f32[2,81,256]{2,1,0:T(8,128)S(1)}, f32[81,256]{1,0:T(8,128)S(1)}, f32[81,256]{1,0:T(8,128)S(1)}) custom-call(f32[1296,128]{1,0:T(8,128)S(1)} %bitcast.4, f32[81,2,256]{2,1,0:T(2,128)S(1)} %bitcast.5, s32[8,128]{1,0:T(8,128)S(1)} %copy-done.4, s32[4]{0:T(128)S(1)} %copy-done.7, s32[4,16]{1,0:T(4,128)S(1)} %copy-done.6, ...), custom_call_target="tpu_custom_call" | custom-call | tf_op jit(solution)/shard_map/pallas_call | solution.py:583
  49.7 1.6 %shard_map.112 = (f32[1296,128]{1,0:T(8,128)}, f32[81,2,256]{2,1,0:T(2,128)}, f32[81,256]{1,0:T(8,128)}, f32[81,256]{1,0:T(8,128)}) custom-call(f32[1296,128]{1,0:T(8,128)S(1)} %get-tuple-element.12.parent_ref, f32[2,81,256]{2,1,0:T(8,128)S(1)} %get-tuple-element.13.nest_ref, f32[81,256]{1,0:T(8,128)S(1)} %get-tuple-element.14.mean_ref, ...), custom_call_target="tpu_custom_call" | custom-call | tf_op jit(solution)/shard_map/pallas_call | solution.py:621
Async XLA Ops:
  0.6 0.7 %copy-start.6 = (s32[4,16]{1,0:T(4,128)S(1)}, s32[4,16]{1,0:T(4,128)}, u32[]{:S(2)}) copy-start(s32[4,16]{1,0:T(4,128)} %bound_ref.1) | copy-start | bytes 772
  0.6 0.7 %copy-start.7 = (s32[4]{0:T(128)S(1)}, s32[4]{0:T(128)}, u32[]{:S(2)}) copy-start(s32[4]{0:T(128)} %shift_ref.1) | copy-start | bytes 52
  1.3 1.1 %copy-start = (f32[2,81,8,128]{3,2,1,0:T(8,128)S(1)}, f32[2,81,8,128]{3,2,1,0:T(8,128)}, u32[]{:S(2)}) copy-start(f32[2,81,8,128]{3,2,1,0:T(8,128)} %param.8) | copy-start | bytes 1990660
  2.4 1.0 %copy-start.1 = (bf16[1056,128]{1,0:T(8,128)(2,1)S(1)}, bf16[1056,128]{1,0:T(8,128)(2,1)}, u32[]{:S(2)}) copy-start(bf16[1056,128]{1,0:T(8,128)(2,1)} %constant.5.clone.parts_ref) | copy-start | bytes 811012
  3.4 0.9 %copy-start.2 = (f32[2,81,256]{2,0,1:T(2,128)S(1)}, f32[2,81,256]{2,0,1:T(2,128)}, u32[]{:S(2)}) copy-start(f32[2,81,256]{2,0,1:T(2,128)} %param.9) | copy-start | bytes 497668
  4.3 0.8 %copy-start.3 = (f32[88,81]{1,0:T(8,128)S(1)}, f32[88,81]{1,0:T(8,128)}, u32[]{:S(2)}) copy-start(f32[88,81]{1,0:T(8,128)} %constant.4.clone.last_ref) | copy-start | bytes 85540
  5.1 0.7 %copy-start.4 = (s32[8,128]{1,0:T(8,128)S(1)}, s32[8,128]{1,0:T(8,128)}, u32[]{:S(2)}) copy-start(s32[8,128]{1,0:T(8,128)} %terrain_ref.1) | copy-start | bytes 12292
  5.8 0.7 %copy-start.5 = (s32[4,256]{1,0:T(4,128)S(1)}, s32[4,256]{1,0:T(4,128)}, u32[]{:S(2)}) copy-start(s32[4,256]{1,0:T(4,128)} %dest_ref.1) | copy-start | bytes 12292

commit v4 on v3

--- a/solution.py
+++ b/solution.py
@@ -157,6 +157,7 @@
 PARTS = 3
 SUB = 16
 EDGE = 8
+WRITES = 2
 
 
 def inverse_powers(levels):
@@ -201,8 +202,10 @@
 
 def fused(
     dims,
-    parent_ref, nest_ref, terrain_ref, shift_ref, bound_ref, dest_ref, last_ref, parts_ref,
-    parent_out, nest_out, mean_out, var_out,
+    parent_in, nest_in, terrain_in, shift_ref, bound_in, dest_in, last_in, parts_in,
+    parent_hbm, nest_out, mean_out, var_out,
+    parent_ref, nest_ref, terrain_ref, bound_ref, dest_ref, last_ref, parts_ref, in_s,
+    parent_out, out_s,
     meta, halo_out, halo_in, terr_in, zg, pm, pr, w, msg, got, mine, theirs,
     meta_s, meta_r, halo_s, halo_r, terr_s, terr_r, z_s, z_r, p_s, p_r, msg_s, msg_r, mem_s, mem_r,
 ):
@@ -231,21 +234,21 @@
         pl.semaphore_signal(barrier, inc=1, device_id=(core, at(d)), device_id_type=MESH)
     pl.semaphore_signal(barrier, inc=1, device_id=(1 - core, me), device_id_type=MESH)
 
-    meta[me, 0:STEPS, :] = dest_ref[...]
-    meta[me, STEPS : 2 * STEPS, :] = jnp.zeros((STEPS, cols), jnp.int32)
-    for s in range(STEPS):
-        index = bound_ref[s : s + 1, :]
-        at_col = lax.rem(lax.rem(index, width) + shift_ref[s] + width, width)
-        meta[me, STEPS + s : STEPS + s + 1, 0:nb] = (index // width) * width + at_col
-
-    for m in range(members):
-        zg[my_z, m] = nn(last_ref[...], nest_ref[:, m, :], HI)
+    sources_in = (parent_in, dest_in, bound_in, terrain_in, nest_in, last_in, parts_in)
+    places_in = (parent_ref, dest_ref, bound_ref, terrain_ref, nest_ref, last_ref, parts_ref)
+    fetches = [
+        pltpu.make_async_copy(a, b, in_s.at[i])
+        for i, (a, b) in enumerate(zip(sources_in, places_in))
+    ]
+    for fetch in fetches:
+        fetch.start()
 
     tail = jnp.zeros((w.shape[3] - EDGE - padded + EDGE, width), F32)
     for t in range(STEPS):
         for r in range(tall):
             for m in range(members):
                 w[t, r, m, padded:, :] = tail
+    fetches[0].wait()
     for r in range(rows):
         for m in range(members):
             w[0, half + r, m, EDGE : EDGE + levels, :] = parent_ref[
@@ -262,6 +265,15 @@
             if d == 0:
                 halo_out[i, half * both :, :] = (field - near.astype(F32)).astype(BF16)
 
+    for fetch in fetches[1:4]:
+        fetch.wait()
+    meta[me, 0:STEPS, :] = dest_ref[...]
+    meta[me, STEPS : 2 * STEPS, :] = jnp.zeros((STEPS, cols), jnp.int32)
+    for s in range(STEPS):
+        index = bound_ref[s : s + 1, :]
+        at_col = lax.rem(lax.rem(index, width) + shift_ref[s] + width, width)
+        meta[me, STEPS + s : STEPS + s + 1, 0:nb] = (index // width) * width + at_col
+
     pl.semaphore_wait(barrier, tiles)
 
     pending = []
@@ -269,9 +281,6 @@
     def start(copy):
         copy.start()
         pending.append(copy)
-
-    for d in range(1, tiles):
-        start(rcopy(meta.at[me], meta.at[me], meta_s.at[d], meta_r.at[d], at(d)))
 
     def halo_pair(i, tile):
         return (
@@ -287,8 +296,16 @@
             for copy in halo_pair(i, to[i]):
                 copy.start()
 
-    for d in range(1, zs):
-        start(rcopy(zg.at[my_z], zg.at[my_z], z_s.at[d], z_r.at[d], at(d * PLANE)))
+    for d in range(1, tiles):
+        start(rcopy(meta.at[me], meta.at[me], meta_s.at[d], meta_r.at[d], at(d)))
+
+    for fetch in fetches[4:]:
+        fetch.wait()
+    for m in range(members):
+        zg[my_z, m] = nn(last_ref[...], nest_ref[:, m, :], HI)
+        for d in range(1, zs):
+            block = zg.at[my_z, m]
+            start(rcopy(block, block, z_s.at[m, d], z_r.at[m, d], at(d * PLANE)))
 
     for d in range(1, tiles):
         rcopy(meta.at[me], meta.at[at(tiles - d)], meta_s.at[d], meta_r.at[d], me).wait_recv()
@@ -343,6 +360,24 @@
         path = hop if path is None else nn(path, hop).astype(BF16)
         moves[s] = path
 
+    def masked(origin, m):
+        out = jnp.zeros((padded, cols), F32)
+        for z in range(zs):
+            out = jnp.where(origin == z * PLANE + my_p, zg[z, m], out)
+        return out
+
+    finals = [my_z * PLANE + lax.rem(my_p + d, PLANE) for d in range(PLANE)]
+    origins = [sources[0]] + [chase(final)[0][0] for final in finals[1:]]
+
+    def second_leg(m):
+        for d in range(1, zs):
+            sent = zg.at[my_z, m]
+            came = zg.at[lax.rem(my_z + zs - d, zs), m]
+            rcopy(sent, came, z_s.at[m, d], z_r.at[m, d], me).wait_recv()
+        for d in range(1, PLANE):
+            pm[d - 1, m] = masked(origins[d], m)
+            start(rcopy(pm.at[d - 1, m], pr.at[d - 1, m], p_s.at[m, d], p_r.at[m, d], finals[d]))
+
     lane_s = lax.rem(lax.broadcasted_iota(jnp.int32, (both, LANES), 1), slot_rows) // CAPB
     picked = [jnp.zeros((both, LANES), F32)]
 
@@ -404,6 +439,8 @@
         for r in range(half + t + 1, half + rows - t - 1):
             advance(t, r)
 
+    second_leg(0)
+
     def outer(t):
         inner = range(half + t + 1, half + rows - t - 1)
         for r in range(t + 1, tall - t - 1):
@@ -434,23 +471,7 @@
     outer(0)
     pick(1)
 
-    for d in range(1, zs):
-        rcopy(
-            zg.at[my_z], zg.at[lax.rem(my_z + zs - d, zs)], z_s.at[d], z_r.at[d], me
-        ).wait_recv()
-
-    def masked(origin, m):
-        out = jnp.zeros((padded, cols), F32)
-        for z in range(zs):
-            out = jnp.where(origin == z * PLANE + my_p, zg[z, m], out)
-        return out
-
-    for d in range(1, PLANE):
-        final = my_z * PLANE + lax.rem(my_p + d, PLANE)
-        origin = chase(final)[0][0]
-        for m in range(members):
-            pm[d - 1, m] = masked(origin, m)
-        start(rcopy(pm.at[d - 1], pr.at[d - 1], p_s.at[d], p_r.at[d], final))
+    second_leg(1)
 
     for t in range(2, STEPS):
         outer(t - 1)
@@ -469,10 +490,13 @@
 
     for r in range(half, half + rows):
         advance(STEPS - 1, r)
+    keep = pltpu.make_async_copy(parent_out, parent_hbm, out_s)
+    keep.start()
 
     origin = sources[0]
     for d in range(1, PLANE):
-        rcopy(pm.at[d - 1], pr.at[d - 1], p_s.at[d], p_r.at[d], me).wait_recv()
+        for m in range(members):
+            rcopy(pm.at[d - 1, m], pr.at[d - 1, m], p_s.at[m, d], p_r.at[m, d], me).wait_recv()
     result = []
     for m in range(members):
         block = masked(origin, m)
@@ -530,7 +554,7 @@
             added = jnp.concatenate([added, jnp.zeros((padded, cols - LANES), F32)], axis=1)
         full = result[m] + added
         mine[m] = full
-        nest_out[m] = full[:levels]
+        nest_out[:, m, :] = full[:levels]
 
     pair = rcopy(mine, theirs, mem_s, mem_r, me, 1 - core)
     pair.start()
@@ -542,6 +566,7 @@
     mean_out[...] = mean
     var_out[...] = functools.reduce(lambda a, b: a + b, [(f - mean) ** 2 for f in fields]) / count
 
+    keep.wait()
     for copy in pending:
         copy.wait_send()
     for i in range(2):
@@ -552,15 +577,18 @@
 
 
 def write_out(parent_ref, nest_ref, mean_ref, var_ref, parent_out, nest_out, mean_out, var_out, sems):
+    piece = parent_ref.shape[0] // WRITES
     copies = [
-        pltpu.make_async_copy(parent_ref, parent_out, sems.at[0]),
-        pltpu.make_async_copy(mean_ref, mean_out, sems.at[1]),
-        pltpu.make_async_copy(var_ref, var_out, sems.at[2]),
+        pltpu.make_async_copy(
+            parent_ref.at[pl.ds(i * piece, piece)], parent_out.at[pl.ds(i * piece, piece)], sems.at[i]
+        )
+        for i in range(WRITES)
     ]
+    others = ((nest_ref, nest_out), (mean_ref, mean_out), (var_ref, var_out))
+    for i, (source, place) in enumerate(others):
+        copies.append(pltpu.make_async_copy(source, place, sems.at[WRITES + i]))
     for copy in copies:
         copy.start()
-    for m in range(nest_ref.shape[0]):
-        nest_out[:, m, :] = nest_ref[m]
     for copy in copies:
         copy.wait()
 
@@ -578,19 +606,30 @@
     both = members * padded
     dims = (members, levels, rows, width, cols, nb, tiles, cols // (tiles // 2), cells)
     vmem = pl.BlockSpec(memory_space=pltpu.VMEM)
+    hbm = pl.BlockSpec(memory_space=pl.ANY)
     dma = pltpu.SemaphoreType.DMA
     last, parts = inverse_powers(levels)
     outs = pl.pallas_call(
         functools.partial(fused, dims),
         out_shape=(
             jax.ShapeDtypeStruct((mixed * rows, width), F32),
-            jax.ShapeDtypeStruct((members, levels, cols), F32),
+            jax.ShapeDtypeStruct((levels, members, cols), F32),
             jax.ShapeDtypeStruct((levels, cols), F32),
             jax.ShapeDtypeStruct((levels, cols), F32),
         ),
-        in_specs=[vmem, vmem, vmem, pl.BlockSpec(memory_space=pltpu.SMEM)] + [vmem] * 4,
-        out_specs=(vmem,) * 4,
+        in_specs=[hbm] * 3 + [pl.BlockSpec(memory_space=pltpu.SMEM)] + [hbm] * 4,
+        out_specs=(hbm, vmem, vmem, vmem),
         scratch_shapes=[
+            pltpu.VMEM((mixed * rows, width), F32),
+            pltpu.VMEM((levels, members, cols), F32),
+            pltpu.VMEM((rows, width), jnp.int32),
+            pltpu.VMEM((STEPS, nb), jnp.int32),
+            pltpu.VMEM((STEPS, cols), jnp.int32),
+            pltpu.VMEM(last.shape, F32),
+            pltpu.VMEM(parts.shape, BF16),
+            dma((7,)),
+            pltpu.VMEM((mixed * rows, width), F32),
+            dma,
             pltpu.VMEM((tiles, 2 * STEPS, cols), jnp.int32),
             pltpu.VMEM((2, (rows // 2 + 1) * both, width), BF16),
             pltpu.VMEM((2, (rows // 2 + 1) * both, width), BF16),
@@ -605,19 +644,19 @@
             pltpu.VMEM((members, padded, cols), F32),
             dma((tiles,)), dma((tiles,)),
             dma((2,)), dma((2,)), dma((2,)), dma((2,)),
-            dma((zs,)), dma((zs,)), dma((PLANE,)), dma((PLANE,)),
+            dma((members, zs)), dma((members, zs)),
+            dma((members, PLANE)), dma((members, PLANE)),
             dma((tiles,)), dma((tiles,)),
             dma, dma,
         ],
         compiler_params=pltpu.CompilerParams(
-            collective_id=0, has_side_effects=True, vmem_limit_bytes=32 * 1024 * 1024
+            collective_id=0, has_side_effects=True, vmem_limit_bytes=62 * 1024 * 1024
         ),
     )(
         parent_state.reshape(mixed * rows, width),
         jnp.transpose(nest_state, (1, 0, 2)), terrain, shift_x, boundary_index, reloc_dest,
         jnp.asarray(last), jnp.asarray(parts),
     )
-    hbm = pl.BlockSpec(memory_space=pl.ANY)
     outs = pl.pallas_call(
         write_out,
         out_shape=(
@@ -626,10 +665,10 @@
             jax.ShapeDtypeStruct((levels, cols), F32),
             jax.ShapeDtypeStruct((levels, cols), F32),
         ),
-        in_specs=[vmem] * 4,
-        out_specs=(hbm, vmem, hbm, hbm),
-        scratch_shapes=[dma((3,))],
-        compiler_params=pltpu.CompilerParams(vmem_limit_bytes=16 * 1024 * 1024),
+        in_specs=[hbm] * 4,
+        out_specs=(hbm,) * 4,
+        scratch_shapes=[dma((WRITES + 3,))],
+        compiler_params=pltpu.CompilerParams(vmem_limit_bytes=62 * 1024 * 1024),
     )(*outs)
     nest_field = jnp.transpose(outs[1], (1, 0, 2))
     return (outs[0].reshape(parent_state.shape), nest_field, outs[2], outs[3])

time: 51.6 us -> 76.3 us (1.48)
  the two profiles are of different devices: /device:TPU:15 before, /device:TPU:0 now
where the time goes in v4:
time: 76.3 us; the launch traced here: 76.2 us
  Pallas kernels  75.5 us (99%)
    pallas_call x1, Pallas kernels, on_device_fused(): pl.pallas_call(functools.partial(fused, dims), out_shape=(jax.ShapeDtypeS...  43.8 us
    pallas_call x1, Pallas kernels, on_device_fused(): pl.pallas_call(write_out, out_shape=(jax.ShapeDtypeStruct((mixed * rows,...  31.7 us

profile of v4, /device:TPU:0, one launch (start us, length us, event | category | flops | bytes accessed | tf_op | source)
XLA Modules:
  0.0 76.2 jit_solution(13719297298789638393)
XLA Ops:
  0.6 43.8 %shard_map.111 = (f32[1296,128]{1,0:T(8,128)}, f32[81,2,256]{2,1,0:T(2,128)}, f32[81,256]{1,0:T(8,128)}, f32[81,256]{1,0:T(8,128)}) custom-call(f32[1296,128]{1,0:T(8,128)} %bitcast.4, f32[81,2,256]{2,1,0:T(2,128)} %bitcast.5, s32[8,128]{1,0:T(8,128)} %terrain_in.1, s32[4]{0:T(128)} %shift_ref.1, s32[4,16]{1,0:T(4,128)} %bound_in.1, s32[4,256]{1,0:T(4,128)} %dest_in.1, ...), custom_call_target="tpu_custom_call" | custom-call | tf_op jit(solution)/shard_map/pallas_call | solution.py:612
  44.4 31.7 %shard_map.112 = (f32[1296,128]{1,0:T(8,128)}, f32[81,2,256]{2,1,0:T(2,128)}, f32[81,256]{1,0:T(8,128)}, f32[81,256]{1,0:T(8,128)}) custom-call(f32[1296,128]{1,0:T(8,128)} %get-tuple-element.12.parent_ref, f32[81,2,256]{2,1,0:T(2,128)} %get-tuple-element.13.nest_ref, f32[81,256]{1,0:T(8,128)} %get-tuple-element.14.mean_ref, f32[81,256]{1,0:T(8,128)} %get-tuple-element.15.var_ref), custom_call_target="tpu_custom_call" | custom-call | tf_op jit(solution)/shard_map/pallas_call | solution.py:660

commit v5 on v4

--- a/solution.py
+++ b/solution.py
@@ -665,7 +665,7 @@
             jax.ShapeDtypeStruct((levels, cols), F32),
             jax.ShapeDtypeStruct((levels, cols), F32),
         ),
-        in_specs=[hbm] * 4,
+        in_specs=[vmem] * 4,
         out_specs=(hbm,) * 4,
         scratch_shapes=[dma((WRITES + 3,))],
         compiler_params=pltpu.CompilerParams(vmem_limit_bytes=62 * 1024 * 1024),

time: 76.3 us -> 46.8 us (0.61)
  Pallas kernels: 75.5 us -> 46 us
    pallas_call x1, Pallas kernels: 31.7 us -> 2.19 us  [on_device_fused(): pl.pallas_call(write_out, out_shape=(jax.ShapeDtypeStruct((mixed * rows,...]
where the time goes in v5:
time: 46.8 us; the launch traced here: 46.6 us
  Pallas kernels  46 us (98%)
  between operations  0.64 us (1%)
    pallas_call x1, Pallas kernels, on_device_fused(): pl.pallas_call(functools.partial(fused, dims), out_shape=(jax.ShapeDtypeS...  43.8 us
    pallas_call x1, Pallas kernels, on_device_fused(): pl.pallas_call(write_out, out_shape=(jax.ShapeDtypeStruct((mixed * rows,...  2.19 us

profile of v5, /device:TPU:0, one launch (start us, length us, event | category | flops | bytes accessed | tf_op | source)
XLA Modules:
  0.0 46.6 jit_solution(13480363888433969803)
XLA Ops:
  0.6 43.8 %shard_map.111 = (f32[1296,128]{1,0:T(8,128)}, f32[81,2,256]{2,1,0:T(2,128)}, f32[81,256]{1,0:T(8,128)}, f32[81,256]{1,0:T(8,128)}) custom-call(f32[1296,128]{1,0:T(8,128)} %bitcast.4, f32[81,2,256]{2,1,0:T(2,128)} %bitcast.5, s32[8,128]{1,0:T(8,128)} %terrain_in.1, s32[4]{0:T(128)} %shift_ref.1, s32[4,16]{1,0:T(4,128)} %bound_in.1, s32[4,256]{1,0:T(4,128)} %dest_in.1, ...), custom_call_target="tpu_custom_call" | custom-call | tf_op jit(solution)/shard_map/pallas_call | solution.py:612
  44.4 2.2 %shard_map.112 = (f32[1296,128]{1,0:T(8,128)}, f32[81,2,256]{2,1,0:T(2,128)}, f32[81,256]{1,0:T(8,128)}, f32[81,256]{1,0:T(8,128)}) custom-call(f32[1296,128]{1,0:T(8,128)} %get-tuple-element.12.parent_ref, f32[81,2,256]{2,1,0:T(2,128)} %get-tuple-element.13.nest_ref, f32[81,256]{1,0:T(8,128)} %get-tuple-element.14.mean_ref, f32[81,256]{1,0:T(8,128)} %get-tuple-element.15.var_ref), custom_call_target="tpu_custom_call" | custom-call | tf_op jit(solution)/shard_map/pallas_call | solution.py:660
